TPU v7x, 32 devices: a whole 2x2x4 slice. The times are simulated.
32 devices in a mesh: dp: 8 (over z, x), tensor: 4 (over y, core).
Axes of the slice: x: 2, y: 2, z: 4, core: 2. Of those that a mesh axis runs over, the one named last changes fastest.
Arguments:
- tokens: bfloat16 [16, 1024, 1024], P('dp', 'tensor'), may hold values from -6 to 6
- lengths: int32 [16, 4], P('dp'), may hold values from 60 to 800, as said below
- ln_attn: bfloat16 [1024], P('dp'), may hold values from 0.099609375 to 1.8984375
- w_query: bfloat16 [1024, 1024], P('dp', 'tensor'), may hold values from -0.1875 to 0.1875
- w_key: bfloat16 [1024, 512], P('dp', 'tensor'), may hold values from -0.1875 to 0.1875
- w_value: bfloat16 [1024, 512], P('dp', 'tensor'), may hold values from -0.1875 to 0.1875
- q_gain: bfloat16 [64], P('dp'), may hold values from 0.099609375 to 1.8984375
- k_gain: bfloat16 [64], P('dp'), may hold values from 0.099609375 to 1.8984375
- w_out: bfloat16 [1024, 1024], P('tensor', 'dp'), may hold values from -1.5 to 1.5
- ln_ffn: bfloat16 [1024], P('dp'), may hold values from 0.099609375 to 1.8984375
- w_gate: bfloat16 [1024, 4608], P('dp', 'tensor'), may hold values from -0.1875 to 0.1875
- w_up: bfloat16 [1024, 4608], P('dp', 'tensor'), may hold values from -0.1875 to 0.1875
- w_down: bfloat16 [4608, 1024], P('tensor', 'dp'), may hold values from -0.09375 to 0.09375
- out_grad: bfloat16 [16, 1024, 1024], P('dp', 'tensor'), may hold values from -6 to 6
Outputs:
- block_out: bfloat16 [16, 1024, 1024], P('dp', 'tensor')
- tokens_grad: float32 [16, 1024, 1024], P('dp', 'tensor')
- ln_attn_grad: float32 [1024], P('dp')
- w_query_grad: float32 [1024, 1024], P('dp', 'tensor')
- w_key_grad: float32 [1024, 512], P('dp', 'tensor')
- w_value_grad: float32 [1024, 512], P('dp', 'tensor')
- q_gain_grad: float32 [64], P('dp')
- k_gain_grad: float32 [64], P('dp')
- w_out_grad: float32 [1024, 1024], P('tensor', 'dp')
- ln_ffn_grad: float32 [1024], P('dp')
- w_gate_grad: float32 [1024, 4608], P('dp', 'tensor')
- up_weight_gradient: float32 [1024, 4608], P('dp', 'tensor')
- w_down_grad: float32 [4608, 1024], P('tensor', 'dp')
Inputs may be any that keep to these rules, and one draw needn't show every extreme that they name: Row s lists the lengths of the 4 documents packed into sequence s, in order; each row sums to 1024, each document has at least 60 tokens, and exactly one document of each row has 800 tokens.
All inputs are finite; a program needn't handle non-finite values.
Results may differ from a plain program's by a relative error of at most 0.019.
Values may be sent and summed in bfloat16 or wider, within the bound.
A program may use at most 192 MiB of HBM per device.

v0:
```python
import jax
import jax.numpy as jnp
from jax import lax
from jax.sharding import PartitionSpec as P

EPSILON = 1e-05
THETA = 1000000.0
MASKED = -1e30


def rms_scale(values, gain_vec):
    return (
        values * lax.rsqrt(jnp.mean(values * values, axis=-1, keepdims=True) + EPSILON) * gain_vec
    )


def doc_tables(lengths, seq_len):
    doc_ends = jnp.cumsum(lengths, axis=-1, dtype=jnp.int32)
    doc_starts = doc_ends - lengths
    positions = jnp.arange(seq_len, dtype=jnp.int32)
    doc_ids = jnp.sum(
        (positions[None, :, None] >= doc_ends[:, None, :]).astype(jnp.int32),
        axis=-1,
        dtype=jnp.int32,
    )
    numbers = jnp.arange(lengths.shape[-1], dtype=jnp.int32)
    opening = jnp.sum(
        jnp.where(doc_ids[:, :, None] == numbers[None, None, :], doc_starts[:, None, :], 0),
        axis=-1,
        dtype=jnp.int32,
    )
    return (doc_ids, positions[None, :] - opening)


def rotary(values, positions):
    half_dim = values.shape[-1] // 2
    freq_rate = jnp.power(THETA, -2.0 * jnp.arange(half_dim, dtype=jnp.float32) / values.shape[-1])
    angles = positions.astype(jnp.float32)[:, :, None, None] * freq_rate
    cosine = jnp.cos(angles)
    sine_part = jnp.sin(angles)
    front_half = values[..., :half_dim]
    back_half = values[..., half_dim:]
    return jnp.concatenate(
        [front_half * cosine - back_half * sine_part, back_half * cosine + front_half * sine_part],
        axis=-1,
    )


def allowed_mask(doc_ids):
    places = jnp.arange(doc_ids.shape[0], dtype=jnp.int32)
    return (doc_ids[:, None] == doc_ids[None, :]) & (places[None, :] <= places[:, None])


def project(matmul_operand, weight_matrix):
    return jnp.einsum(
        "xpo,oh->xph", matmul_operand, weight_matrix, preferred_element_type=jnp.float32
    )


def project_back(gradient_term, weight_matrix):
    return jnp.einsum(
        "yhp,np->yhn", gradient_term, weight_matrix, preferred_element_type=jnp.float32
    )


def weight_grad(matmul_operand, gradient_term):
    return jnp.einsum(
        "wba,wbh->ah", matmul_operand, gradient_term, preferred_element_type=jnp.float32
    )


def score_block(queries, key_rows, doc_ids):
    seq_len, heads, head_dim = queries.shape
    key_value_heads = key_rows.shape[1]
    grouped = queries.reshape(seq_len, key_value_heads, heads // key_value_heads, head_dim)
    scores = jnp.einsum(
        "qkgd,tkd->kgqt", grouped, key_rows, preferred_element_type=jnp.float32
    ) * head_dim ** (-0.5)
    return (grouped, jnp.where(allowed_mask(doc_ids), scores, MASKED))


def attend_forward(packed):
    queries, key_rows, value_rows, doc_ids = packed
    seq_len = queries.shape[0]
    grouped, scores = score_block(queries, key_rows, doc_ids)
    row_max = jnp.max(scores, axis=-1, keepdims=True)
    exp_scores = jnp.exp(scores - row_max)
    row_total = jnp.sum(exp_scores, axis=-1, keepdims=True)
    probs = (exp_scores / row_total).astype(jnp.bfloat16)
    mixture = jnp.einsum("kgqt,tkd->qkgd", probs, value_rows, preferred_element_type=jnp.float32)
    return (mixture.reshape(seq_len, -1).astype(jnp.bfloat16), row_max + jnp.log(row_total))


def attend_backward(packed):
    queries, key_rows, value_rows, doc_ids, log_total, mix_grad = packed
    seq_len, heads, head_dim = queries.shape
    key_value_heads = key_rows.shape[1]
    grouped, scores = score_block(queries, key_rows, doc_ids)
    probs = jnp.exp(scores - log_total)
    mix_grouped = mix_grad.reshape(seq_len, key_value_heads, heads // key_value_heads, head_dim)
    prob_grad = jnp.einsum(
        "qkgd,tkd->kgqt", mix_grouped, value_rows, preferred_element_type=jnp.float32
    )
    value_grad = jnp.einsum(
        "kgqt,qkgd->tkd",
        probs.astype(jnp.bfloat16),
        mix_grouped,
        preferred_element_type=jnp.float32,
    )
    score_grad = (probs * (prob_grad - jnp.sum(probs * prob_grad, axis=-1, keepdims=True))).astype(
        jnp.bfloat16
    )
    score_scale = head_dim ** (-0.5)
    query_grad = (
        jnp.einsum("kgqt,tkd->qkgd", score_grad, key_rows, preferred_element_type=jnp.float32)
        * score_scale
    )
    key_grad = (
        jnp.einsum("kgqt,qkgd->tkd", score_grad, grouped, preferred_element_type=jnp.float32)
        * score_scale
    )
    return (query_grad.reshape(seq_len, heads, head_dim), key_grad, value_grad.astype(jnp.bfloat16))


def on_device(
    tokens,
    lengths,
    ln_attn,
    w_query,
    w_key,
    w_value,
    q_gain,
    k_gain,
    w_out,
    ln_ffn,
    w_gate,
    w_up,
    w_down,
    out_grad,
):
    gathered = (
        lax.all_gather(ln_attn, "dp", axis=0, tiled=True),
        lax.all_gather(w_query, "dp", axis=0, tiled=True),
        lax.all_gather(w_key, "dp", axis=0, tiled=True),
        lax.all_gather(w_value, "dp", axis=0, tiled=True),
        lax.all_gather(q_gain, "dp", axis=0, tiled=True),
        lax.all_gather(k_gain, "dp", axis=0, tiled=True),
        lax.all_gather(w_out, "dp", axis=1, tiled=True),
        lax.all_gather(ln_ffn, "dp", axis=0, tiled=True),
        lax.all_gather(w_gate, "dp", axis=0, tiled=True),
        lax.all_gather(w_up, "dp", axis=0, tiled=True),
        lax.all_gather(w_down, "dp", axis=1, tiled=True),
    )
    (
        attn_gain,
        query_weight,
        key_weight,
        value_weight,
        query_gain,
        key_gain,
        out_weight,
        ffn_gain,
        gate_weight,
        up_weight,
        down_weight,
    ) = gathered
    head_dim = query_gain.shape[0]
    inputs = tokens.astype(jnp.float32)
    normed = lax.all_gather(
        rms_scale(inputs, attn_gain.astype(jnp.float32)).astype(jnp.bfloat16),
        "tensor",
        axis=1,
        tiled=True,
    )
    seq_count, seq_len = (normed.shape[0], normed.shape[1])
    doc_ids, positions = doc_tables(lengths, seq_len)

    def query_side(raw_heads, gain_vec):
        return rotary(rms_scale(raw_heads, gain_vec), positions)

    query_raw = project(normed, query_weight).reshape(seq_count, seq_len, -1, head_dim)
    key_raw = project(normed, key_weight).reshape(seq_count, seq_len, -1, head_dim)
    queries = query_side(query_raw, query_gain.astype(jnp.float32)).astype(jnp.bfloat16)
    key_rows = query_side(key_raw, key_gain.astype(jnp.float32)).astype(jnp.bfloat16)
    value_rows = (
        project(normed, value_weight).astype(jnp.bfloat16).reshape(seq_count, seq_len, -1, head_dim)
    )
    mixture, log_total = lax.map(attend_forward, (queries, key_rows, value_rows, doc_ids))
    attn_out = lax.psum_scatter(
        project(mixture, out_weight).astype(jnp.bfloat16), "tensor", scatter_dimension=1, tiled=True
    ).astype(jnp.float32)
    mid_stream = inputs + attn_out
    normed_mid = lax.all_gather(
        rms_scale(mid_stream, ffn_gain.astype(jnp.float32)).astype(jnp.bfloat16),
        "tensor",
        axis=1,
        tiled=True,
    )
    gate_proj = project(normed_mid, gate_weight)
    up_proj = project(normed_mid, up_weight)
    hidden = (jax.nn.silu(gate_proj) * up_proj).astype(jnp.bfloat16)
    ffn_out = lax.psum_scatter(
        project(hidden, down_weight).astype(jnp.bfloat16), "tensor", scatter_dimension=1, tiled=True
    ).astype(jnp.float32)
    block_out = (mid_stream + ffn_out).astype(jnp.bfloat16)
    weights_back = (
        lax.all_gather(ln_attn, "dp", axis=0, tiled=True),
        lax.all_gather(w_query, "dp", axis=0, tiled=True),
        lax.all_gather(w_key, "dp", axis=0, tiled=True),
        lax.all_gather(w_value, "dp", axis=0, tiled=True),
        lax.all_gather(q_gain, "dp", axis=0, tiled=True),
        lax.all_gather(k_gain, "dp", axis=0, tiled=True),
        lax.all_gather(w_out, "dp", axis=1, tiled=True),
        lax.all_gather(ln_ffn, "dp", axis=0, tiled=True),
        lax.all_gather(w_gate, "dp", axis=0, tiled=True),
        lax.all_gather(w_up, "dp", axis=0, tiled=True),
        lax.all_gather(w_down, "dp", axis=1, tiled=True),
    )
    (
        attn_gain,
        query_weight,
        key_weight,
        value_weight,
        query_gain,
        key_gain,
        out_weight,
        ffn_gain,
        gate_weight,
        up_weight,
        down_weight,
    ) = weights_back
    grad_full = lax.all_gather(out_grad, "tensor", axis=1, tiled=True)
    down_grad = weight_grad(hidden, grad_full)
    hidden_grad = project_back(grad_full, down_weight)
    silu_pull = jax.vjp(
        lambda gate_part, up_part: jax.nn.silu(gate_part) * up_part, gate_proj, up_proj
    )[1]
    gate_grad, up_grad = silu_pull(hidden_grad)
    gate_grad = gate_grad.astype(jnp.bfloat16)
    up_grad = up_grad.astype(jnp.bfloat16)
    gate_w_grad = weight_grad(normed_mid, gate_grad)
    up_w_grad = weight_grad(normed_mid, up_grad)
    mid_norm_grad = lax.psum_scatter(
        (project_back(gate_grad, gate_weight) + project_back(up_grad, up_weight)).astype(
            jnp.bfloat16
        ),
        "tensor",
        scatter_dimension=1,
        tiled=True,
    ).astype(jnp.float32)
    mid_pull = jax.vjp(rms_scale, mid_stream, ffn_gain.astype(jnp.float32))[1]
    stream_grad, ffn_gain_grad = mid_pull(mid_norm_grad)
    mid_grad = out_grad.astype(jnp.float32) + stream_grad
    mid_low = lax.all_gather(mid_grad.astype(jnp.bfloat16), "tensor", axis=1, tiled=True)
    out_w_grad = weight_grad(mixture, mid_low)
    mix_grad = project_back(mid_low, out_weight).astype(jnp.bfloat16)
    query_grad, key_grad, value_grad = lax.map(
        attend_backward, (queries, key_rows, value_rows, doc_ids, log_total, mix_grad)
    )
    query_pull = jax.vjp(query_side, query_raw, query_gain.astype(jnp.float32))[1]
    query_raw_grad, query_gain_grad = query_pull(query_grad)
    key_pull = jax.vjp(query_side, key_raw, key_gain.astype(jnp.float32))[1]
    key_raw_grad, key_gain_grad = key_pull(key_grad)
    query_low = query_raw_grad.reshape(seq_count, seq_len, -1).astype(jnp.bfloat16)
    key_lower_bound = key_raw_grad.reshape(seq_count, seq_len, -1).astype(jnp.bfloat16)
    value_low = value_grad.reshape(seq_count, seq_len, -1)
    query_w_grad = weight_grad(normed, query_low)
    key_w_grad = weight_grad(normed, key_lower_bound)
    value_w_grad = weight_grad(normed, value_low)
    input_terms = (
        project_back(query_low, query_weight)
        + project_back(key_lower_bound, key_weight)
        + project_back(value_low, value_weight)
    )
    input_norm_grad = lax.psum_scatter(
        input_terms.astype(jnp.bfloat16), "tensor", scatter_dimension=1, tiled=True
    ).astype(jnp.float32)
    input_pull = jax.vjp(rms_scale, inputs, attn_gain.astype(jnp.float32))[1]
    input_grad, attn_gain_grad = input_pull(input_norm_grad)
    tokens_grad = mid_grad + input_grad
    gain_totals = lax.psum(
        (attn_gain_grad, query_gain_grad, key_gain_grad, ffn_gain_grad), "tensor"
    )
    summed = (
        lax.psum_scatter(gain_totals[0], "dp", scatter_dimension=0, tiled=True),
        lax.psum_scatter(query_w_grad, "dp", scatter_dimension=0, tiled=True),
        lax.psum_scatter(key_w_grad, "dp", scatter_dimension=0, tiled=True),
        lax.psum_scatter(value_w_grad, "dp", scatter_dimension=0, tiled=True),
        lax.psum_scatter(gain_totals[1], "dp", scatter_dimension=0, tiled=True),
        lax.psum_scatter(gain_totals[2], "dp", scatter_dimension=0, tiled=True),
        lax.psum_scatter(out_w_grad, "dp", scatter_dimension=1, tiled=True),
        lax.psum_scatter(gain_totals[3], "dp", scatter_dimension=0, tiled=True),
        lax.psum_scatter(gate_w_grad, "dp", scatter_dimension=0, tiled=True),
        lax.psum_scatter(up_w_grad, "dp", scatter_dimension=0, tiled=True),
        lax.psum_scatter(down_grad, "dp", scatter_dimension=1, tiled=True),
    )
    return (block_out, tokens_grad) + tuple(summed)


def solution(mesh):
    in_specs = (
        P("dp", "tensor", None),
        P("dp", None),
        P("dp"),
        P("dp", "tensor"),
        P("dp", "tensor"),
        P("dp", "tensor"),
        P("dp"),
        P("dp"),
        P("tensor", "dp"),
        P("dp"),
        P("dp", "tensor"),
        P("dp", "tensor"),
        P("tensor", "dp"),
        P("dp", "tensor", None),
    )
    out_specs = (
        P("dp", "tensor", None),
        P("dp", "tensor", None),
        P("dp"),
        P("dp", "tensor"),
        P("dp", "tensor"),
        P("dp", "tensor"),
        P("dp"),
        P("dp"),
        P("tensor", "dp"),
        P("dp"),
        P("dp", "tensor"),
        P("dp", "tensor"),
        P("tensor", "dp"),
    )
    return jax.shard_map(
        on_device, mesh=mesh, in_specs=in_specs, out_specs=out_specs, check_vma=False
    )
```

profile of v0, /device:TPU:0, one launch (start us, length us, event | category | flops | bytes accessed | tf_op | source)
XLA Modules:
  0.0 1329.8 jit_solution(8668374898991575004)
XLA Ops:
  9.7 22.3 %all-gather = bf16[8,1,128]{2,1,0:T(2,128)(2,1)S(1)} all-gather(bf16[1,1,128]{2,1,0:T(2,128)(2,1)} %bitcast.320), channel_id=1, replica_groups=mesh['dp'=8,'tensor'=4] {'dp'}, dimensions={0}, use_global_device_ids=true | all-gather | bytes 2304 | tf_op jit(solution)/shard_map/all_gather | solution.py:142
  37.0 17.1 %all-reduce.12 = (bf16[64]{0:T(256)(128)(2,1)S(1)}, bf16[64]{0:T(256)(128)(2,1)S(1)}) all-reduce(bf16[64]{0:T(256)(128)(2,1)S(1)} %dynamic-update-slice, bf16[64]{0:T(256)(128)(2,1)S(1)} %dynamic-update-slice.1), channel_id=1, replica_groups=mesh['dp'=8,'tensor'=4] {'dp'}, use_global_device_ids=true, to_apply=%add.4 | all-reduce | flops 128 | bytes 512
  55.0 26.7 %all_gather.58 = bf16[1024,128]{0,1:T(8,128)(2,1)S(1)} all-gather(bf16[128,128]{0,1:T(8,128)(2,1)S(1)} %copy.79), channel_id=1, replica_groups=mesh['dp'=8,'tensor'=4] {'dp'}, dimensions={0}, use_global_device_ids=true | all-gather | bytes 294912 | tf_op jit(solution)/shard_map/all_gather | solution.py:145
  81.6 26.4 %all_gather.59 = bf16[1024,128]{0,1:T(8,128)(2,1)S(1)} all-gather(bf16[128,128]{0,1:T(8,128)(2,1)S(1)} %copy.80), channel_id=1, replica_groups=mesh['dp'=8,'tensor'=4] {'dp'}, dimensions={0}, use_global_device_ids=true | all-gather | bytes 294912 | tf_op jit(solution)/shard_map/all_gather | solution.py:144
  108.1 27.7 %all_gather.61 = bf16[1024,256]{0,1:T(8,128)(2,1)S(1)} all-gather(bf16[128,256]{0,1:T(8,128)(2,1)S(1)} %copy.81), channel_id=1, replica_groups=mesh['dp'=8,'tensor'=4] {'dp'}, dimensions={0}, use_global_device_ids=true | all-gather | bytes 589824 | tf_op jit(solution)/shard_map/all_gather | solution.py:143
  135.8 28.1 %all_gather.63 = bf16[256,1024]{1,0:T(8,128)(2,1)} all-gather(bf16[256,128]{1,0:T(8,128)(2,1)S(1)} %copy-done.53), channel_id=1, replica_groups=mesh['dp'=8,'tensor'=4] {'dp'}, dimensions={1}, use_global_device_ids=true | all-gather | bytes 589824 | tf_op jit(solution)/shard_map/all_gather | solution.py:148
  173.8 27.3 %while.26 = (s32[]{:T(128)}, bf16[2,1024,256]{1,2,0:T(8,128)(2,1)}, f32[2,2,2,1024,1]{3,2,1,4,0:T(2,128)S(1)}, bf16[2,1024,2,64]{1,3,2,0:T(8,128)(2,1)S(1)}, s32...) while((s32[]{:T(128)}, bf16[2,1024,256]{1,2,0:T(8,128)(2,1)}, ...), condition=%wide.region_9.10_spmd, body=%wide.region_6.9_spmd.sunk | while | flops 1127477248 | bytes 66728108 | solution.py:188
  181.5 5.0 fusion.159
  195.0 5.0 fusion.159
  201.9 4.7 convolution_convert_fusion.1
  207.3 16.2 %all-gather.1 = bf16[8,1,128]{2,1,0:T(2,128)(2,1)S(1)} all-gather(bf16[1,1,128]{2,1,0:T(2,128)(2,1)S(1)} %bitcast.321), channel_id=1, replica_groups=mesh['dp'=8,'tensor'=4] {'dp'}, dimensions={0}, use_global_device_ids=true | all-gather | bytes 2304 | tf_op jit(solution)/shard_map/all_gather | solution.py:149
  223.5 25.7 %reduce-scatter.12.cloned.1.call-done = bf16[2,256,1024]{2,1,0:T(8,128)(2,1)} async-done(((bf16[2,1024,1024]{2,1,0:T(8,128)(2,1)}), bf16[2,256,1024]{2,1,0:T(8,128)(2,1)}) %reduce-scatter.12.cloned.1.call-update) | async-done | bytes 1048592 | tf_op jit(solution)/shard_map/reduce_scatter | solution.py:189
  259.0 35.0 %all-gather.12.cloned.1.call-done = bf16[2,1024,1024]{2,1,0:T(8,128)(2,1)} async-done(((bf16[2,256,1024]{2,1,0:T(8,128)(2,1)}), bf16[2,1024,1024]{2,1,0:T(8,128)(2,1)}) %all-gather.12.cloned.1.call-update) | async-done | bytes 4194320 | tf_op jit(solution)/shard_map/all_gather | solution.py:193
  294.0 10.7 fusion.64
  304.7 43.4 %all-gather.14.cloned.1.call-done = bf16[1024,1152]{1,0:T(8,128)(2,1)} async-done(((bf16[128,1152]{1,0:T(8,128)(2,1)}), bf16[1024,1152]{1,0:T(8,128)(2,1)}) %all-gather.14.cloned.1.call-update) | async-done | bytes 2359312 | tf_op jit(solution)/shard_map/all_gather | solution.py:150
  348.1 10.3 fusion.68
  358.4 44.1 %all-gather.18.cloned.1.call-done = bf16[1152,1024]{1,0:T(8,128)(2,1)} async-done(((bf16[1152,128]{1,0:T(8,128)(2,1)}), bf16[1152,1024]{1,0:T(8,128)(2,1)}) %all-gather.18.cloned.1.call-update) | async-done | bytes 2359312 | tf_op jit(solution)/shard_map/all_gather | solution.py:152
  402.6 34.2 %all-gather.20.cloned.1.call-done = bf16[2,1024,1024]{2,1,0:T(8,128)(2,1)} async-done(((bf16[2,256,1024]{2,1,0:T(8,128)(2,1)}), bf16[2,1024,1024]{2,1,0:T(8,128)(2,1)}) %all-gather.20.cloned.1.call-update) | async-done | bytes 4194320 | tf_op jit(solution)/shard_map/all_gather | solution.py:232
  436.8 16.7 %multiply_convert_fusion = (bf16[2,1024,1152]{2,1,0:T(8,128)(2,1)}, bf16[2,1024,1152]{2,1,0:T(8,128)(2,1)}, bf16[2,1024,1152]{2,1,0:T(8,128)(2,1)}) fusion(f32[2,1024,1152]{2,1,0:T(8,128)} %fusion.68, f32[2,1024,1152]{2,1,0:T(8,128)} %fusion.64, bf16[2,1024,1024]{2,1,0:T(8,128)(2,1)} %all-gather.20.cloned.1.call-done, ...), kind=kOutput, calls=%fused_computation.66 | convolution fusion | flops 4869586944 | bytes 39583744 | tf_op jit(solution)/shard_map/yhp,np->yhn/dot_general | solution.py:61
  453.5 7.7 fusion.66
  461.2 7.6 add_convert_fusion.1
  468.8 44.6 %reduce-scatter.16.cloned.1.call-done = bf16[2,256,1024]{2,1,0:T(8,128)(2,1)} async-done(((bf16[2,1024,1024]{2,1,0:T(8,128)(2,1)}), bf16[2,256,1024]{2,1,0:T(8,128)(2,1)}) %reduce-scatter.16.cloned.1.call-update) | async-done | bytes 1048592 | tf_op jit(solution)/shard_map/reduce_scatter | solution.py:243
  519.7 34.6 %all-gather.22.cloned.1.call-done = bf16[2,1024,1024]{2,1,0:T(8,128)(2,1)} async-done(((bf16[2,256,1024]{2,1,0:T(8,128)(2,1)}), bf16[2,1024,1024]{2,1,0:T(8,128)(2,1)}) %all-gather.22.cloned.1.call-update) | async-done | bytes 4194320 | tf_op jit(solution)/shard_map/all_gather | solution.py:254
  557.9 96.3 %while.27 = (s32[]{:T(128)}, f32[2,1024,4,64]{1,3,2,0:T(8,128)}, f32[2,1024,2,64]{1,3,2,0:T(8,128)}, bf16[2,1024,2,64]{1,3,2,0:T(8,128)(2,1)}, bf16[2,1024,2,64]...) while((s32[]{:T(128)}, f32[2,1024,4,64]{1,3,2,0:T(8,128)}, ...), condition=%wide.region_17.18_spmd, body=%wide.region_15.17_spmd.sunk | while | flops 2750935040 | bytes 241103568 | solution.py:257
  560.8 8.2 fusion.169
  569.0 8.9 fusion.174
  577.9 13.6 %fusion.171 = (f32[2,2,1024]{2,1,0:T(2,128)}, f32[2,1024,1024,2]{2,1,3,0:T(8,128)}) fusion(f32[2,1024,1024,2]{2,1,3,0:T(8,128)} %fusion.169, f32[2,2,1024]{2,1,0:T(2,128)} %dynamic-slice_bitcast_fusion.2, pred[1024,1024]{0,1:T(8,128)(4,1)S(1)} %fusion.170, bf16[1024,2,2,64]{0,3,2,1:T(8,128)(2,1)} %bitcast.300, ...), kind=kOutput, calls=%fused_computation.24.clone.1 | convolution fusion | flops 557838336 | bytes 35422212 | tf_op jit(solution)/shard_map/while/body/eval_jaxpr/qkgd,tkd->kgqt/dot_general | solution.py:101
  591.6 8.4 fusion.172
  608.7 8.2 fusion.169
  616.9 8.9 fusion.174
  625.9 13.6 %fusion.171 = (f32[2,2,1024]{2,1,0:T(2,128)}, f32[2,1024,1024,2]{2,1,3,0:T(8,128)}) fusion(f32[2,1024,1024,2]{2,1,3,0:T(8,128)} %fusion.169, f32[2,2,1024]{2,1,0:T(2,128)} %dynamic-slice_bitcast_fusion.2, pred[1024,1024]{0,1:T(8,128)(4,1)S(1)} %fusion.170, bf16[1024,2,2,64]{0,3,2,1:T(8,128)(2,1)} %bitcast.300, ...), kind=kOutput, calls=%fused_computation.24.clone.1 | convolution fusion | flops 557838336 | bytes 35422212 | tf_op jit(solution)/shard_map/while/body/eval_jaxpr/qkgd,tkd->kgqt/dot_general | solution.py:101
  639.5 8.4 fusion.172
  669.5 9.6 convolution_convert_fusion
  679.2 9.8 convolution_bitcast_fusion.1
  689.1 10.6 convolution_bitcast_fusion.2
  699.7 10.3 convolution_bitcast_fusion.3
  710.1 4.4 convolution_bitcast_fusion.6
  719.1 5.1 convolution_bitcast_fusion.4
  724.3 5.2 convolution_bitcast_fusion.5
  733.1 21.9 %all-reduce.10 = (f32[1024]{0:T(1024)S(1)}, f32[64]{0:T(128)S(1)}, f32[64]{0:T(128)S(1)}, f32[1024]{0:T(1024)S(1)}) all-reduce(f32[1024]{0:T(1024)S(1)} %get-tuple-element.144, f32[64]{0:T(128)S(1)} %get-tuple-element.142, f32[64]{0:T(128)S(1)} %get-tuple-element.146, ...), channel_id=6, replica_groups=mesh['dp'=8,'tensor'=4] {'dp'}, use_global_device_ids=true, to_apply=%region_24.25.clone | all-reduce | flops 2176 | bytes 17408
  755.3 6.4 all-reduce.11
  766.1 93.3 %reduce-scatter.32.cloned.1.call-done = f32[1152,128]{1,0:T(8,128)} async-done(((f32[1152,1024]{1,0:T(8,128)}), f32[1152,128]{1,0:T(8,128)}) %reduce-scatter.32.cloned.1.call-update) | async-done | bytes 589840 | tf_op jit(solution)/shard_map/reduce_scatter | solution.py:295
  859.3 98.9 %reduce-scatter.30.cloned.1.call-done = f32[128,1152]{1,0:T(8,128)} async-done(((f32[1024,1152]{1,0:T(8,128)}), f32[128,1152]{1,0:T(8,128)}) %reduce-scatter.30.cloned.1.call-update) | async-done | bytes 589840 | tf_op jit(solution)/shard_map/reduce_scatter | solution.py:294
  958.2 99.1 %reduce-scatter.28.cloned.1.call-done = f32[128,1152]{1,0:T(8,128)} async-done(((f32[1024,1152]{1,0:T(8,128)}), f32[128,1152]{1,0:T(8,128)}) %reduce-scatter.28.cloned.1.call-update) | async-done | bytes 589840 | tf_op jit(solution)/shard_map/reduce_scatter | solution.py:293
  1057.3 65.5 %reduce-scatter.24.cloned.1.call-done = f32[128,128]{1,0:T(8,128)} async-done(((f32[1024,128]{1,0:T(8,128)}), f32[128,128]{1,0:T(8,128)}) %reduce-scatter.24.cloned.1.call-update) | async-done | bytes 65552 | tf_op jit(solution)/shard_map/reduce_scatter | solution.py:288
  1122.8 65.4 %reduce-scatter.22.cloned.1.call-done = f32[128,128]{1,0:T(8,128)} async-done(((f32[1024,128]{1,0:T(8,128)}), f32[128,128]{1,0:T(8,128)}) %reduce-scatter.22.cloned.1.call-update) | async-done | bytes 65552 | tf_op jit(solution)/shard_map/reduce_scatter | solution.py:287
  1188.2 66.9 %reduce-scatter.26.cloned.1.call-done = f32[256,128]{1,0:T(8,128)} async-done(((f32[256,1024]{1,0:T(8,128)}), f32[256,128]{1,0:T(8,128)}) %reduce-scatter.26.cloned.1.call-update) | async-done | bytes 131088 | tf_op jit(solution)/shard_map/reduce_scatter | solution.py:291
  1255.1 66.9 %reduce-scatter.20.cloned.1.call-done = f32[128,256]{1,0:T(8,128)} async-done(((f32[1024,256]{1,0:T(8,128)}), f32[128,256]{1,0:T(8,128)}) %reduce-scatter.20.cloned.1.call-update) | async-done | bytes 131088 | tf_op jit(solution)/shard_map/reduce_scatter | solution.py:286
  (346 shorter events, 98.2 us)
Async XLA Ops:
  8.0 27.2 %copy-start.71 = (u32[32]{0:T(128)S(1)}, u32[32]{0:T(128)}, u32[]{:S(2)}) copy-start(u32[32]{0:T(128)} %constant.110) | copy-start | bytes 388
  8.0 28.5 %copy-start.76 = (bf16[8]{0:T(256)(128)(2,1)S(1)}, bf16[8]{0:T(256)(128)(2,1)}, u32[]{:S(2)}) copy-start(bf16[8]{0:T(256)(128)(2,1)} %param.25) | copy-start | bytes 52
  8.0 28.7 %copy-start.77 = (bf16[8]{0:T(256)(128)(2,1)S(1)}, bf16[8]{0:T(256)(128)(2,1)}, u32[]{:S(2)}) copy-start(bf16[8]{0:T(256)(128)(2,1)} %param.24) | copy-start | bytes 52
  8.0 46.1 %copy-start.70 = (s32[2,4]{1,0:T(2,128)S(1)}, s32[2,4]{1,0:T(2,128)}, u32[]{:S(2)}) copy-start(s32[2,4]{1,0:T(2,128)} %param.19) | copy-start | bytes 100
  8.1 46.3 %copy-start.57 = (bf16[128,128]{1,0:T(8,128)(2,1)S(1)}, bf16[128,128]{1,0:T(8,128)(2,1)}, u32[]{:S(2)}) copy-start(bf16[128,128]{1,0:T(8,128)(2,1)} %param.22) | copy-start | bytes 98308
  8.1 46.4 %copy-start.58 = (bf16[128,128]{1,0:T(8,128)(2,1)S(1)}, bf16[128,128]{1,0:T(8,128)(2,1)}, u32[]{:S(2)}) copy-start(bf16[128,128]{1,0:T(8,128)(2,1)} %param.23) | copy-start | bytes 98308
  8.1 46.5 %copy-start.54 = (bf16[128,256]{1,0:T(8,128)(2,1)S(1)}, bf16[128,256]{1,0:T(8,128)(2,1)}, u32[]{:S(2)}) copy-start(bf16[128,256]{1,0:T(8,128)(2,1)} %param.21) | copy-start | bytes 196612
  8.1 127.7 %copy-start.53 = (bf16[256,128]{1,0:T(8,128)(2,1)S(1)}, bf16[256,128]{1,0:T(8,128)(2,1)}, u32[]{:S(2)}) copy-start(bf16[256,128]{1,0:T(8,128)(2,1)} %param.26) | copy-start | bytes 196612
  8.1 156.8 %all-gather.10.cloned.1.call-start = ((), (), s32[]{:S(2)}) async-start(), calls=%async_computation.11 | async-start | bytes 5242880 | tf_op jit(solution)/shard_map/all_gather | solution.py:169
  9.7 44.8 %copy-start.63 = (f32[2,256]{1,0:T(2,128)}, f32[2,256]{1,0:T(2,128)S(1)}, u32[]{:S(2)}) copy-start(f32[2,256]{1,0:T(2,128)S(1)} %fusion.77) | copy-start | bytes 6148
  9.7 44.8 %copy-start.59 = (f32[2,256]{1,0:T(2,128)}, f32[2,256]{1,0:T(2,128)S(1)}, u32[]{:S(2)}) copy-start(f32[2,256]{1,0:T(2,128)S(1)} %fusion.95) | copy-start | bytes 6148
  35.1 214.1 %reduce-scatter.12.cloned.1.call-start = ((), (), s32[]{:S(2)}) async-start(), calls=%async_computation.12 | async-start | bytes 5242880 | tf_op jit(solution)/shard_map/reduce_scatter | solution.py:189
  54.1 116.2 %copy-start.66 = (f32[64]{0:T(128)}, f32[64]{0:T(128)S(1)}, u32[]{:S(2)}) copy-start(f32[64]{0:T(128)S(1)} %convert_element_type.136) | copy-start | bytes 772
  54.1 116.7 %copy-start.68 = (f32[64]{0:T(128)}, f32[64]{0:T(128)S(1)}, u32[]{:S(2)}) copy-start(f32[64]{0:T(128)S(1)} %convert_element_type.138) | copy-start | bytes 772
  81.6 90.7 %copy-start.28 = (bf16[1024,128]{0,1:T(8,128)(2,1)}, bf16[1024,128]{0,1:T(8,128)(2,1)S(1)}, u32[]{:S(2)}) copy-start(bf16[1024,128]{0,1:T(8,128)(2,1)S(1)} %all_gather.58) | copy-start | bytes 786436
  108.1 62.2 %copy-start.30 = (bf16[1024,128]{0,1:T(8,128)(2,1)}, bf16[1024,128]{0,1:T(8,128)(2,1)S(1)}, u32[]{:S(2)}) copy-start(bf16[1024,128]{0,1:T(8,128)(2,1)S(1)} %all_gather.59) | copy-start | bytes 786436
  135.8 34.5 %copy-start.32 = (bf16[1024,256]{0,1:T(8,128)(2,1)}, bf16[1024,256]{0,1:T(8,128)(2,1)S(1)}, u32[]{:S(2)}) copy-start(bf16[1024,256]{0,1:T(8,128)(2,1)S(1)} %all_gather.61) | copy-start | bytes 1572868
  173.8 28.1 %copy-start.36 = (bf16[256,1024]{1,0:T(8,128)(2,1)S(1)}, bf16[256,1024]{1,0:T(8,128)(2,1)}, u32[]{:S(2)}) copy-start(bf16[256,1024]{1,0:T(8,128)(2,1)} %all_gather.63) | copy-start | bytes 1572868
  201.9 47.3 %copy-start.3 = (bf16[2,256,1024]{2,1,0:T(8,128)(2,1)S(1)}, bf16[2,256,1024]{2,1,0:T(8,128)(2,1)}, u32[]{:S(2)}) copy-start(bf16[2,256,1024]{2,1,0:T(8,128)(2,1)} %param.18) | copy-start | bytes 3145732
  206.7 52.3 %all-gather.16.cloned.1.call-start = ((), (), s32[]{:S(2)}) async-start(), calls=%async_computation.15 | async-start | bytes 2654208 | tf_op jit(solution)/shard_map/all_gather | solution.py:151
  207.3 86.7 %all-gather.12.cloned.1.call-start = ((), (), s32[]{:S(2)}) async-start(), calls=%async_computation.13 | async-start | bytes 5242880 | tf_op jit(solution)/shard_map/all_gather | solution.py:193
  223.5 292.7 %copy-start.49 = (f32[8,1,128]{2,1,0:T(1,128)}, f32[8,1,128]{2,1,0:T(1,128)S(1)}, u32[]{:S(2)}) copy-start(f32[8,1,128]{2,1,0:T(1,128)S(1)} %convert_element_type.161) | copy-start | bytes 12292
  250.9 265.4 %copy-start.55 = (f32[2,256]{1,0:T(2,128)}, f32[2,256]{1,0:T(2,128)S(1)}, u32[]{:S(2)}) copy-start(f32[2,256]{1,0:T(2,128)S(1)} %fusion.96) | copy-start | bytes 6148
  253.5 94.6 %all-gather.14.cloned.1.call-start = ((), (), s32[]{:S(2)}) async-start(), calls=%async_computation.14 | async-start | bytes 2654208 | tf_op jit(solution)/shard_map/all_gather | solution.py:150
  254.1 148.5 %all-gather.18.cloned.1.call-start = ((), (), s32[]{:S(2)}) async-start(), calls=%async_computation.16 | async-start | bytes 2654208 | tf_op jit(solution)/shard_map/all_gather | solution.py:152
  254.8 181.9 %all-gather.20.cloned.1.call-start = ((), (), s32[]{:S(2)}) async-start(), calls=%async_computation.18 | async-start | bytes 5242880 | tf_op jit(solution)/shard_map/all_gather | solution.py:232
  255.6 257.9 %reduce-scatter.16.cloned.1.call-start = ((), (), s32[]{:S(2)}) async-start(), calls=%async_computation.19 | async-start | bytes 5242880 | tf_op jit(solution)/shard_map/reduce_scatter | solution.py:243
  468.7 44.7 %copy-start.10 = (bf16[2,256,1024]{2,1,0:T(8,128)(2,1)S(1)}, bf16[2,256,1024]{2,1,0:T(8,128)(2,1)}, u32[]{:S(2)}) copy-start(bf16[2,256,1024]{2,1,0:T(8,128)(2,1)} %reduce-scatter.12.cloned.1.call-done) | copy-start | bytes 3145732
  468.8 85.5 %all-gather.22.cloned.1.call-start = ((), (), s32[]{:S(2)}) async-start(), calls=%async_computation.20 | async-start | bytes 5242880 | tf_op jit(solution)/shard_map/all_gather | solution.py:254
  516.3 41.6 %copy-start.61 = (f32[2,256]{1,0:T(2,128)}, f32[2,256]{1,0:T(2,128)S(1)}, u32[]{:S(2)}) copy-start(f32[2,256]{1,0:T(2,128)S(1)} %multiply_multiply_fusion.5) | copy-start | bytes 6148
  519.6 38.3 %copy-start.15 = (bf16[2,1024,2,64]{1,3,2,0:T(8,128)(2,1)S(1)}, bf16[2,1024,2,64]{1,3,2,0:T(8,128)(2,1)}, u32[]{:S(2)}) copy-start(bf16[2,1024,2,64]{1,3,2,0:T(8,128)(2,1)} %copy-done.14) | copy-start | bytes 1572868
  519.6 211.2 %reduce-scatter.18.cloned.1.call-start = ((), (), s32[]{:S(2)}) async-start(), calls=%async_computation.21 | async-start | bytes 5242880 | tf_op jit(solution)/shard_map/reduce_scatter | solution.py:275
  616.9 22.6 %slice-start = ((s8[16777216]{0:T(1024)(128)(4,1)}), s8[4194304]{0:T(1024)(128)(4,1)S(1)}, s32[]{:S(2)}) async-start(s8[16777216]{0:T(1024)(128)(4,1)} %bitcast.295), calls=%async_computation.29 | async-start | bytes 8388608 | tf_op jit(solution)/shard_map/while
  616.9 22.6 %slice-start.1 = ((s8[16777216]{0:T(1024)(128)(4,1)}), s8[4194304]{0:T(1024)(128)(4,1)S(1)}, s32[]{:S(2)}) async-start(s8[16777216]{0:T(1024)(128)(4,1)} %bitcast.295), calls=%async_computation.30 | async-start | bytes 8388608 | tf_op jit(solution)/shard_map/while
  667.9 93.9 %reduce-scatter.14.cloned.1.call-start = ((), (), s32[]{:S(2)}) async-start(), calls=%async_computation.17 | async-start | bytes 5242880 | tf_op jit(solution)/shard_map/reduce_scatter | solution.py:202
  679.2 180.2 %reduce-scatter.32.cloned.1.call-start = ((), (), s32[]{:S(2)}) async-start(), calls=%async_computation.28 | async-start | bytes 5308416 | tf_op jit(solution)/shard_map/reduce_scatter | solution.py:295
  689.0 269.2 %reduce-scatter.30.cloned.1.call-start = ((), (), s32[]{:S(2)}) async-start(), calls=%async_computation.27 | async-start | bytes 5308416 | tf_op jit(solution)/shard_map/reduce_scatter | solution.py:294
  699.7 357.7 %reduce-scatter.28.cloned.1.call-start = ((), (), s32[]{:S(2)}) async-start(), calls=%async_computation.26 | async-start | bytes 5308416 | tf_op jit(solution)/shard_map/reduce_scatter | solution.py:293
  710.1 412.8 %reduce-scatter.24.cloned.1.call-start = ((), (), s32[]{:S(2)}) async-start(), calls=%async_computation.24 | async-start | bytes 589824 | tf_op jit(solution)/shard_map/reduce_scatter | solution.py:288
  714.6 473.7 %reduce-scatter.22.cloned.1.call-start = ((), (), s32[]{:S(2)}) async-start(), calls=%async_computation.23 | async-start | bytes 589824 | tf_op jit(solution)/shard_map/reduce_scatter | solution.py:287
  719.0 536.1 %reduce-scatter.26.cloned.1.call-start = ((), (), s32[]{:S(2)}) async-start(), calls=%async_computation.25 | async-start | bytes 1179648 | tf_op jit(solution)/shard_map/reduce_scatter | solution.py:291
  724.2 37.6 %copy-start.64 = (f32[2,256]{1,0:T(2,128)S(1)}, f32[2,256]{1,0:T(2,128)}, u32[]{:S(2)}) copy-start(f32[2,256]{1,0:T(2,128)} %copy-done.63) | copy-start | bytes 6148
  724.2 37.6 %copy-start.11 = (bf16[2,256,1024]{2,1,0:T(8,128)(2,1)S(1)}, bf16[2,256,1024]{2,1,0:T(8,128)(2,1)}, u32[]{:S(2)}) copy-start(bf16[2,256,1024]{2,1,0:T(8,128)(2,1)} %reduce-scatter.12.cloned.1.call-done) | copy-start | bytes 3145732
  724.2 37.6 %copy-start.17 = (bf16[2,256,1024]{2,1,0:T(8,128)(2,1)S(1)}, bf16[2,256,1024]{2,1,0:T(8,128)(2,1)}, u32[]{:S(2)}) copy-start(bf16[2,256,1024]{2,1,0:T(8,128)(2,1)} %param.31) | copy-start | bytes 3145732
  724.2 37.6 %copy-start.50 = (f32[8,1,128]{2,1,0:T(1,128)S(1)}, f32[8,1,128]{2,1,0:T(1,128)}, u32[]{:S(2)}) copy-start(f32[8,1,128]{2,1,0:T(1,128)} %copy-done.49) | copy-start | bytes 12292
  724.3 37.6 %copy-start.56 = (f32[2,256]{1,0:T(2,128)S(1)}, f32[2,256]{1,0:T(2,128)}, u32[]{:S(2)}) copy-start(f32[2,256]{1,0:T(2,128)} %copy-done.55) | copy-start | bytes 6148
  724.3 37.6 %copy-start.62 = (f32[2,256]{1,0:T(2,128)S(1)}, f32[2,256]{1,0:T(2,128)}, u32[]{:S(2)}) copy-start(f32[2,256]{1,0:T(2,128)} %copy-done.61) | copy-start | bytes 6148
  724.3 597.7 %reduce-scatter.20.cloned.1.call-start = ((), (), s32[]{:S(2)}) async-start(), calls=%async_computation.22 | async-start | bytes 1179648 | tf_op jit(solution)/shard_map/reduce_scatter | solution.py:286
  (74 other events, 364.0 us)
Sparse Core Ops, SparseCore 0:
  35.2 31.7 all-gather.9
  206.8 42.3 reduce-scatter.11
  468.9 44.5 reduce-scatter.15
  519.8 34.4 all-gather.21
Sparse Core Ops, SparseCore 1:
  209.4 49.6 all-gather.15
  261.1 32.8 all-gather.11
  296.3 51.7 all-gather.13
  350.3 52.2 all-gather.17
  404.2 32.5 all-gather.19
  668.0 44.4 reduce-scatter.17
  715.0 44.4 reduce-scatter.13
  763.5 95.7 reduce-scatter.31
  863.4 94.8 reduce-scatter.29
  962.5 94.8 reduce-scatter.27
  1061.1 61.7 reduce-scatter.23
  1127.1 61.0 reduce-scatter.21
  1192.1 62.9 reduce-scatter.25
  1259.5 62.5 reduce-scatter.19
where the time goes:
time: 1340 us; the launch traced here: 1330 us
  waiting for transfers between devices  824 us (61%)
  matrix products  220 us (16%)
  blocking collectives  193 us (14%)
  other arithmetic  56.2 us (4%)
  between operations  19.1 us (1%)
  local copies, waits for them, and re-layouts  15.6 us (1%)
    reduce_scatter x1, waiting for transfers between devices, on_device(): lax.psum_scatter(gate_w_grad, 'dp', scatter_dimension=0, tiled=True)  99.1 us
    reduce_scatter x1, waiting for transfers between devices, on_device(): lax.psum_scatter(up_w_grad, 'dp', scatter_dimension=0, tiled=True)  98.9 us
    reduce_scatter x1, waiting for transfers between devices, on_device(): lax.psum_scatter(down_grad, 'dp', scatter_dimension=1, tiled=True)  93.3 us
    reduce_scatter x1, waiting for transfers between devices, on_device(): lax.psum_scatter(query_w_grad, 'dp', scatter_dimension=0, tiled=True)  66.9 us
    reduce_scatter x1, waiting for transfers between devices, on_device(): lax.psum_scatter(out_w_grad, 'dp', scatter_dimension=1, tiled=True)  66.9 us
    reduce_scatter x1, waiting for transfers between devices, on_device(): lax.psum_scatter(value_w_grad, 'dp', scatter_dimension=0, tiled=True)  65.5 us
    reduce_scatter x1, waiting for transfers between devices, on_device(): lax.psum_scatter(key_w_grad, 'dp', scatter_dimension=0, tiled=True)  65.4 us
    dot_general x7, matrix products, weight_grad(): jnp.einsum('wba,wbh->ah', matmul_operand, gradient_term, preferred_elemen...  49.8 us
  transfers between devices with their start and end apart: 18, of which 15 were waited for; matrix products, arithmetic and copies ran while one was open for 7% of the time, Pallas kernels for 0%

commit v1 on v0

v1 whole, which is shorter than its diff:
```python
import jax
import jax.numpy as jnp
from jax import lax
from jax.sharding import PartitionSpec as P

EPSILON = 1e-05
THETA = 1000000.0
MASKED = -1e30


def rms_scale(values, gain_vec):
    return (
        values * lax.rsqrt(jnp.mean(values * values, axis=-1, keepdims=True) + EPSILON) * gain_vec
    )


def doc_tables(lengths, seq_len):
    doc_ends = jnp.cumsum(lengths, axis=-1, dtype=jnp.int32)
    doc_starts = doc_ends - lengths
    positions = jnp.arange(seq_len, dtype=jnp.int32)
    doc_ids = jnp.sum(
        (positions[None, :, None] >= doc_ends[:, None, :]).astype(jnp.int32),
        axis=-1,
        dtype=jnp.int32,
    )
    numbers = jnp.arange(lengths.shape[-1], dtype=jnp.int32)
    opening = jnp.sum(
        jnp.where(doc_ids[:, :, None] == numbers[None, None, :], doc_starts[:, None, :], 0),
        axis=-1,
        dtype=jnp.int32,
    )
    return (doc_ids, positions[None, :] - opening)


def rotary(values, positions):
    half_dim = values.shape[-1] // 2
    freq_rate = jnp.power(THETA, -2.0 * jnp.arange(half_dim, dtype=jnp.float32) / values.shape[-1])
    angles = positions.astype(jnp.float32)[:, :, None, None] * freq_rate
    cosine = jnp.cos(angles)
    sine_part = jnp.sin(angles)
    front_half = values[..., :half_dim]
    back_half = values[..., half_dim:]
    return jnp.concatenate(
        [front_half * cosine - back_half * sine_part, back_half * cosine + front_half * sine_part],
        axis=-1,
    )


def allowed_mask(doc_ids):
    places = jnp.arange(doc_ids.shape[0], dtype=jnp.int32)
    return (doc_ids[:, None] == doc_ids[None, :]) & (places[None, :] <= places[:, None])


def project(matmul_operand, weight_matrix):
    return jnp.einsum(
        "xpo,oh->xph", matmul_operand, weight_matrix, preferred_element_type=jnp.float32
    )


def project_back(gradient_term, weight_matrix):
    return jnp.einsum(
        "yhp,np->yhn", gradient_term, weight_matrix, preferred_element_type=jnp.float32
    )


def weight_grad(matmul_operand, gradient_term):
    return jnp.einsum(
        "wba,wbh->ah", matmul_operand, gradient_term, preferred_element_type=jnp.float32
    )


def score_block(queries, key_rows, doc_ids):
    seq_len, heads, head_dim = queries.shape
    key_value_heads = key_rows.shape[1]
    grouped = queries.reshape(seq_len, key_value_heads, heads // key_value_heads, head_dim)
    scores = jnp.einsum(
        "qkgd,tkd->kgqt", grouped, key_rows, preferred_element_type=jnp.float32
    ) * head_dim ** (-0.5)
    return (grouped, jnp.where(allowed_mask(doc_ids), scores, MASKED))


def attend_forward(packed):
    queries, key_rows, value_rows, doc_ids = packed
    seq_len = queries.shape[0]
    grouped, scores = score_block(queries, key_rows, doc_ids)
    row_max = jnp.max(scores, axis=-1, keepdims=True)
    exp_scores = jnp.exp(scores - row_max)
    row_total = jnp.sum(exp_scores, axis=-1, keepdims=True)
    probs = (exp_scores / row_total).astype(jnp.bfloat16)
    mixture = jnp.einsum("kgqt,tkd->qkgd", probs, value_rows, preferred_element_type=jnp.float32)
    return (mixture.reshape(seq_len, -1).astype(jnp.bfloat16), row_max + jnp.log(row_total))


def attend_backward(packed):
    queries, key_rows, value_rows, doc_ids, log_total, mix_grad = packed
    seq_len, heads, head_dim = queries.shape
    key_value_heads = key_rows.shape[1]
    grouped, scores = score_block(queries, key_rows, doc_ids)
    probs = jnp.exp(scores - log_total)
    mix_grouped = mix_grad.reshape(seq_len, key_value_heads, heads // key_value_heads, head_dim)
    prob_grad = jnp.einsum(
        "qkgd,tkd->kgqt", mix_grouped, value_rows, preferred_element_type=jnp.float32
    )
    value_grad = jnp.einsum(
        "kgqt,qkgd->tkd",
        probs.astype(jnp.bfloat16),
        mix_grouped,
        preferred_element_type=jnp.float32,
    )
    score_grad = (probs * (prob_grad - jnp.sum(probs * prob_grad, axis=-1, keepdims=True))).astype(
        jnp.bfloat16
    )
    score_scale = head_dim ** (-0.5)
    query_grad = (
        jnp.einsum("kgqt,tkd->qkgd", score_grad, key_rows, preferred_element_type=jnp.float32)
        * score_scale
    )
    key_grad = (
        jnp.einsum("kgqt,qkgd->tkd", score_grad, grouped, preferred_element_type=jnp.float32)
        * score_scale
    )
    return (query_grad.reshape(seq_len, heads, head_dim), key_grad, value_grad.astype(jnp.bfloat16))


def on_device(
    tokens,
    lengths,
    ln_attn,
    w_query,
    w_key,
    w_value,
    q_gain,
    k_gain,
    w_out,
    ln_ffn,
    w_gate,
    w_up,
    w_down,
    out_grad,
):
    parts = lax.axis_size("dp")
    share = w_query.shape[0]
    width = share * parts
    gain_share = q_gain.shape[0]
    head_dim = gain_share * parts
    q_cols, k_cols, v_cols = (w_query.shape[1], w_key.shape[1], w_value.shape[1])
    qkv_cols = q_cols + k_cols + v_cols
    out_rows = w_out.shape[0]
    hidden_units = w_gate.shape[1]
    gain_cols = jnp.stack(
        [
            ln_attn,
            ln_ffn,
            jnp.pad(q_gain, (0, share - gain_share)),
            jnp.pad(k_gain, (0, share - gain_share)),
        ],
        axis=1,
    )
    attn_pack = jnp.concatenate(
        [w_query, w_key, w_value, w_out.T, jnp.pad(gain_cols, ((0, 0), (0, 124)))], axis=1
    )
    attn_all = lax.all_gather(attn_pack, "dp", axis=0, tiled=True)
    tokens_full = lax.all_gather(tokens, "tensor", axis=1, tiled=True)
    qkv_weight = attn_all[:, :qkv_cols]
    out_weight_t = attn_all[:, qkv_cols : qkv_cols + out_rows]
    gains = attn_all[:, qkv_cols + out_rows : qkv_cols + out_rows + 4].astype(jnp.float32)
    attn_gain = gains[:, 0]
    ffn_gain = gains[:, 1]
    query_gain = gains[:, 2].reshape(parts, share)[:, :gain_share].reshape(-1)
    key_gain = gains[:, 3].reshape(parts, share)[:, :gain_share].reshape(-1)
    ffn_pack = jnp.concatenate([w_gate, w_up, w_down.T], axis=1)
    ffn_all = lax.all_gather(ffn_pack, "dp", axis=0, tiled=True)
    gate_up_weight = ffn_all[:, : 2 * hidden_units]
    down_weight_t = ffn_all[:, 2 * hidden_units :]
    grad_full = lax.all_gather(out_grad, "tensor", axis=1, tiled=True)

    inputs = tokens.astype(jnp.float32)
    normed = rms_scale(tokens_full.astype(jnp.float32), attn_gain).astype(jnp.bfloat16)
    seq_count, seq_len = (normed.shape[0], normed.shape[1])
    doc_ids, positions = doc_tables(lengths, seq_len)

    def query_side(raw_heads, gain_vec):
        return rotary(rms_scale(raw_heads, gain_vec), positions)

    qkv_raw = project(normed, qkv_weight)
    query_raw = qkv_raw[..., :q_cols].reshape(seq_count, seq_len, -1, head_dim)
    key_raw = qkv_raw[..., q_cols : q_cols + k_cols].reshape(seq_count, seq_len, -1, head_dim)
    queries = query_side(query_raw, query_gain).astype(jnp.bfloat16)
    key_rows = query_side(key_raw, key_gain).astype(jnp.bfloat16)
    value_rows = (
        qkv_raw[..., q_cols + k_cols :]
        .astype(jnp.bfloat16)
        .reshape(seq_count, seq_len, -1, head_dim)
    )
    mixture, log_total = lax.map(attend_forward, (queries, key_rows, value_rows, doc_ids))
    attn_out = lax.psum_scatter(
        project_back(mixture, out_weight_t).astype(jnp.bfloat16),
        "tensor",
        scatter_dimension=1,
        tiled=True,
    ).astype(jnp.float32)
    mid_stream = inputs + attn_out
    normed_mid = lax.all_gather(
        rms_scale(mid_stream, ffn_gain).astype(jnp.bfloat16),
        "tensor",
        axis=1,
        tiled=True,
    )
    gate_up = project(normed_mid, gate_up_weight)
    gate_proj = gate_up[..., :hidden_units]
    up_proj = gate_up[..., hidden_units:]
    hidden = (jax.nn.silu(gate_proj) * up_proj).astype(jnp.bfloat16)
    hidden_grad = project(grad_full, down_weight_t)
    silu_pull = jax.vjp(
        lambda gate_part, up_part: jax.nn.silu(gate_part) * up_part, gate_proj, up_proj
    )[1]
    gate_grad, up_grad = silu_pull(hidden_grad)
    gate_up_grad = jnp.concatenate([gate_grad, up_grad], axis=-1).astype(jnp.bfloat16)
    mid_norm_grad = lax.psum_scatter(
        project_back(gate_up_grad, gate_up_weight).astype(jnp.bfloat16),
        "tensor",
        scatter_dimension=1,
        tiled=True,
    ).astype(jnp.float32)
    ffn_sums = project_back(hidden, down_weight_t).astype(jnp.bfloat16)
    ffn_w_grads = jnp.concatenate(
        [weight_grad(normed_mid, gate_up_grad), weight_grad(grad_full, hidden)], axis=1
    ).astype(jnp.bfloat16)
    mid_pull = jax.vjp(rms_scale, mid_stream, ffn_gain)[1]
    stream_grad, ffn_gain_grad = mid_pull(mid_norm_grad)
    mid_grad = out_grad.astype(jnp.float32) + stream_grad
    mid_low = lax.all_gather(mid_grad.astype(jnp.bfloat16), "tensor", axis=1, tiled=True)
    mid_low, ffn_w_grads, ffn_sums = lax.optimization_barrier((mid_low, ffn_w_grads, ffn_sums))
    ffn_summed = lax.psum_scatter(ffn_w_grads, "dp", scatter_dimension=0, tiled=True)
    ffn_out = lax.psum_scatter(ffn_sums, "tensor", scatter_dimension=1, tiled=True)
    block_out = (mid_stream + ffn_out.astype(jnp.float32)).astype(jnp.bfloat16)
    out_w_grad_t = weight_grad(mid_low, mixture)
    mix_grad = project(mid_low, out_weight_t).astype(jnp.bfloat16)
    query_grad, key_grad, value_grad = lax.map(
        attend_backward, (queries, key_rows, value_rows, doc_ids, log_total, mix_grad)
    )
    query_pull = jax.vjp(query_side, query_raw, query_gain)[1]
    query_raw_grad, query_gain_grad = query_pull(query_grad)
    key_pull = jax.vjp(query_side, key_raw, key_gain)[1]
    key_raw_grad, key_gain_grad = key_pull(key_grad)
    qkv_low = jnp.concatenate(
        [
            query_raw_grad.reshape(seq_count, seq_len, -1).astype(jnp.bfloat16),
            key_raw_grad.reshape(seq_count, seq_len, -1).astype(jnp.bfloat16),
            value_grad.reshape(seq_count, seq_len, -1),
        ],
        axis=-1,
    )
    input_norm_grad = lax.psum_scatter(
        project_back(qkv_low, qkv_weight).astype(jnp.bfloat16),
        "tensor",
        scatter_dimension=1,
        tiled=True,
    ).astype(jnp.float32)
    input_pull = jax.vjp(rms_scale, inputs, attn_gain)[1]
    input_grad, attn_gain_grad = input_pull(input_norm_grad)
    tokens_grad = mid_grad + input_grad
    gain_cut = jnp.concatenate(
        [
            attn_gain_grad.reshape(parts, share),
            ffn_gain_grad.reshape(parts, share),
            query_gain_grad.reshape(parts, gain_share),
            key_gain_grad.reshape(parts, gain_share),
        ],
        axis=1,
    )
    attn_w_grads = jnp.concatenate(
        [weight_grad(normed, qkv_low), out_w_grad_t], axis=1
    ).astype(jnp.bfloat16)
    attn_summed = lax.psum_scatter(
        attn_w_grads, "dp", scatter_dimension=0, tiled=True
    ).astype(jnp.float32)
    gain_mine = lax.dynamic_index_in_dim(
        lax.psum(gain_cut, ("dp", "tensor")), lax.axis_index("dp"), axis=0, keepdims=False
    )
    ffn_summed = ffn_summed.astype(jnp.float32)
    return (
        block_out,
        tokens_grad,
        gain_mine[:share],
        attn_summed[:, :q_cols],
        attn_summed[:, q_cols : q_cols + k_cols],
        attn_summed[:, q_cols + k_cols : qkv_cols],
        gain_mine[2 * share : 2 * share + gain_share],
        gain_mine[2 * share + gain_share :],
        attn_summed[:, qkv_cols:].T,
        gain_mine[share : 2 * share],
        ffn_summed[:, :hidden_units],
        ffn_summed[:, hidden_units : 2 * hidden_units],
        ffn_summed[:, 2 * hidden_units :].T,
    )


def solution(mesh):
    in_specs = (
        P("dp", "tensor", None),
        P("dp", None),
        P("dp"),
        P("dp", "tensor"),
        P("dp", "tensor"),
        P("dp", "tensor"),
        P("dp"),
        P("dp"),
        P("tensor", "dp"),
        P("dp"),
        P("dp", "tensor"),
        P("dp", "tensor"),
        P("tensor", "dp"),
        P("dp", "tensor", None),
    )
    out_specs = (
        P("dp", "tensor", None),
        P("dp", "tensor", None),
        P("dp"),
        P("dp", "tensor"),
        P("dp", "tensor"),
        P("dp", "tensor"),
        P("dp"),
        P("dp"),
        P("tensor", "dp"),
        P("dp"),
        P("dp", "tensor"),
        P("dp", "tensor"),
        P("tensor", "dp"),
    )
    return jax.shard_map(
        on_device, mesh=mesh, in_specs=in_specs, out_specs=out_specs, check_vma=False
    )
```

time: 1340 us -> 928 us (0.69)
  waiting for transfers between devices: 824 us -> 562 us
  blocking collectives: 193 us -> 39.7 us
  matrix products: 220 us -> 196 us
  local copies, waits for them, and re-layouts: 15.6 us -> 37.1 us
  other arithmetic: 56.2 us -> 70.9 us
    reduce_scatter x11 -> x5, waiting for transfers between devices: 626 us -> 261 us  [the longest x1 129 us: on_device(): lax.psum_scatter(ffn_w_grads, 'dp', scatter_dimension=0, tiled=True)]
    all_gather x6 -> x0, blocking collectives: 147 us -> none  [the longest x1 28.1 us: on_device(): lax.all_gather(w_out, 'dp', axis=1, tiled=True)]
    all_gather x5 -> x4, waiting for transfers between devices: 126 us -> 222 us  [the longest x1 107 us: on_device(): ffn_all = lax.all_gather(ffn_pack, 'dp', axis=0, tiled=True)]
    unnamed x18 -> x13, waiting for transfers between devices: 2.65 us -> 60.2 us
    unnamed x2 -> x0, blocking collectives: 39 us -> none
    all_gather x1, waiting for transfers between devices: 34.6 us -> 0.01 us  [on_device(): lax.all_gather(mid_grad.astype(jnp.bfloat16), 'tensor', axis=1, tiled=True)]
    psum x1, blocking collectives: 6.44 us -> 39.7 us  [on_device(): lax.psum(gain_cut, ('dp', 'tensor'))]
    dot_general x7 -> x4, matrix products: 49.8 us -> 33.8 us  [weight_grad(): jnp.einsum('wba,wbh->ah', matmul_operand, gradient_term, preferred_elemen...]
  transfers between devices with their start and end apart: 18 -> 12, of which waited for: 15 -> 11; matrix products, arithmetic and copies ran while one was open for 7% -> 9% of each run, Pallas kernels for 0% -> 0%
where the time goes in v1:
time: 928 us; the launch traced here: 923 us
  waiting for transfers between devices  562 us (61%)
  matrix products  196 us (21%)
  other arithmetic  70.9 us (8%)
  blocking collectives  39.7 us (4%)
  local copies, waits for them, and re-layouts  37.1 us (4%)
  between operations  15.2 us (2%)
    reduce_scatter x1, waiting for transfers between devices, on_device(): lax.psum_scatter(ffn_w_grads, 'dp', scatter_dimension=0, tiled=True)  129 us
    all_gather x1, waiting for transfers between devices, on_device(): ffn_all = lax.all_gather(ffn_pack, 'dp', axis=0, tiled=True)  107 us
    unnamed x13, waiting for transfers between devices  60.2 us
    all_gather x1, waiting for transfers between devices, on_device(): attn_all = lax.all_gather(attn_pack, 'dp', axis=0, tiled=True)  47.2 us
    reduce_scatter x1, waiting for transfers between devices, on_device(): lax.psum_scatter(project_back(gate_up_grad, gate_up_weight).astype(jnp.bf...  44.6 us
    reduce_scatter x1, waiting for transfers between devices, on_device(): lax.psum_scatter(project_back(mixture, out_weight_t).astype(jnp.bfloat16)...  42.1 us
    reduce_scatter x1, waiting for transfers between devices, on_device(): lax.psum_scatter(project_back(qkv_low, qkv_weight).astype(jnp.bfloat16),...  40.3 us
    dot_general x4, matrix products, project(): jnp.einsum('xpo,oh->xph', matmul_operand, weight_matrix, preferred_elemen...  40.1 us
  transfers between devices with their start and end apart: 12, of which 11 were waited for; matrix products, arithmetic and copies ran while one was open for 9% of the time, Pallas kernels for 0%

profile of v1, /device:TPU:0, one launch (start us, length us, event | category | flops | bytes accessed | tf_op | source)
XLA Modules:
  0.0 922.5 jit_solution(8431453453664411878)
XLA Ops:
  16.5 47.2 %all-gather.9.cloned.1.call-done = bf16[1024,896]{0,1:T(8,128)(2,1)} async-done(((bf16[128,896]{0,1:T(8,128)(2,1)}), bf16[1024,896]{0,1:T(8,128)(2,1)}) %all-gather.9.cloned.1.call-update) | async-done | bytes 1835024 | tf_op jit(solution)/shard_map/all_gather | solution.py:162
  65.2 32.8 %all-gather.7.cloned.1.call-done = bf16[2,1024,1024]{2,1,0:T(8,128)(2,1)} async-done(((bf16[2,256,1024]{2,1,0:T(8,128)(2,1)}), bf16[2,1024,1024]{2,1,0:T(8,128)(2,1)}) %all-gather.7.cloned.1.call-update) | async-done | bytes 4194320 | tf_op jit(solution)/shard_map/all_gather | solution.py:163
  97.9 3.2 fusion.57
  101.8 3.7 fusion.65
  108.6 27.3 %while.26 = (s32[]{:T(128)}, bf16[2,1024,256]{1,2,0:T(8,128)(2,1)}, f32[2,2,2,1024,1]{3,2,1,4,0:T(2,128)S(1)}, bf16[2,1024,2,64]{1,3,2,0:T(8,128)(2,1)S(1)}, s32...) while((s32[]{:T(128)}, bf16[2,1024,256]{1,2,0:T(8,128)(2,1)}, ...), condition=%wide.region_9.10_spmd, body=%wide.region_6.9_spmd.sunk | while | flops 1127477248 | bytes 66728108 | solution.py:195
  109.6 3.0 fusion.145
  112.6 3.7 fusion.146
  116.3 5.0 fusion.147
  123.0 3.0 fusion.145
  126.1 3.7 fusion.146
  129.8 5.0 fusion.147
  136.6 4.7 convolution_convert_fusion.2
  144.0 42.1 %reduce-scatter.9.cloned.1.call-done = bf16[2,256,1024]{2,1,0:T(8,128)(2,1)} async-done(((bf16[2,1024,1024]{2,1,0:T(8,128)(2,1)}), bf16[2,256,1024]{2,1,0:T(8,128)(2,1)}) %reduce-scatter.9.cloned.1.call-update) | async-done | bytes 1048592 | tf_op jit(solution)/shard_map/reduce_scatter | solution.py:196
  191.0 107.2 %all-gather.11.cloned.1.call-done = bf16[1024,3456]{0,1:T(8,128)(2,1)} async-done(((bf16[128,3456]{0,1:T(8,128)(2,1)}), bf16[1024,3456]{0,1:T(8,128)(2,1)}) %all-gather.11.cloned.1.call-update) | async-done | bytes 7077904 | tf_op jit(solution)/shard_map/all_gather | solution.py:172
  298.3 34.8 %all-gather.15.cloned.1.call-done = bf16[2,1024,1024]{2,1,0:T(8,128)(2,1)} async-done(((bf16[2,256,1024]{2,1,0:T(8,128)(2,1)}), bf16[2,1024,1024]{2,1,0:T(8,128)(2,1)}) %all-gather.15.cloned.1.call-update) | async-done | bytes 4194320 | tf_op jit(solution)/shard_map/all_gather | solution.py:203
  333.0 17.2 %fusion.61 = f32[2,1024,2304]{1,2,0:T(8,128)} fusion(bf16[2,1024,1024]{2,1,0:T(8,128)(2,1)} %all-gather.15.cloned.1.call-done, bf16[1024,3456]{0,1:T(8,128)(2,1)} %all-gather.11.cloned.1.call-done), kind=kOutput, calls=%fused_computation.88 | convolution fusion | flops 9663676416 | bytes 27787264 | tf_op jit(solution)/shard_map/xpo,oh->xph/dot_general | solution.py:55
  350.2 18.8 %all-gather.13.cloned.1.call-done = bf16[2,1024,1024]{2,1,0:T(8,128)(2,1)} async-done(((bf16[2,256,1024]{2,1,0:T(8,128)(2,1)}), bf16[2,1024,1024]{2,1,0:T(8,128)(2,1)}) %all-gather.13.cloned.1.call-update) | async-done | bytes 4194320 | tf_op jit(solution)/shard_map/all_gather | solution.py:175
  369.0 16.9 %fusion.54 = (bf16[2,1024,1152]{1,2,0:T(8,128)(2,1)}, bf16[2,1024,1152]{1,2,0:T(8,128)(2,1)}, bf16[2,1024,1152]{1,2,0:T(8,128)(2,1)}) fusion(f32[2,1024,2304]{1,2,0:T(8,128)} %fusion.61, bf16[2,1024,1024]{2,1,0:T(8,128)(2,1)} %all-gather.13.cloned.1.call-done, bf16[1024,3456]{0,1:T(8,128)(2,1)} %all-gather.11.cloned.1.call-done), kind=kOutput, calls=%fused_computation.67 | convolution fusion | flops 4869586944 | bytes 39583744 | tf_op jit(solution)/shard_map/xpo,oh->xph/dot_general | solution.py:55
  385.9 15.6 %fusion.67 = bf16[2,1024,1024]{2,1,0:T(8,128)(2,1)} fusion(bf16[1024,3456]{0,1:T(8,128)(2,1)} %all-gather.11.cloned.1.call-done, bf16[2,1024,1152]{1,2,0:T(8,128)(2,1)} %get-tuple-element.256, bf16[2,1024,1152]{1,2,0:T(8,128)(2,1)} %get-tuple-element.255), kind=kOutput, calls=%fused_computation.95 | convolution fusion | flops 9684647936 | bytes 18350080 | tf_op jit(solution)/shard_map/yhp,np->yhn/dot_general | solution.py:61
  401.6 44.6 %reduce-scatter.11.cloned.1.call-done = bf16[2,256,1024]{2,1,0:T(8,128)(2,1)} async-done(((bf16[2,1024,1024]{2,1,0:T(8,128)(2,1)}), bf16[2,256,1024]{2,1,0:T(8,128)(2,1)}) %reduce-scatter.11.cloned.1.call-update) | async-done | bytes 1048592 | tf_op jit(solution)/shard_map/reduce_scatter | solution.py:219
  446.2 3.0 fusion.72
  449.2 3.3 fusion.84
  454.9 8.7 fusion.62
  463.6 15.7 %bitcast_convert_fusion = bf16[1024,2304]{1,0:T(8,128)(2,1)} fusion(bf16[2,1024,1024]{2,1,0:T(8,128)(2,1)S(1)} %copy-done.65, bf16[2,1024,1152]{1,2,0:T(8,128)(2,1)} %get-tuple-element.256, bf16[2,1024,1152]{1,2,0:T(8,128)(2,1)} %get-tuple-element.255), kind=kOutput, calls=%fused_computation.69 | convolution fusion | flops 9684910080 | bytes 18350080 | tf_op jit(solution)/shard_map/wba,wbh->ah/dot_general | solution.py:67
  479.3 5.6 pad_maximum_fusion.1
  484.9 10.1 %convolution_convert_fusion.1 = bf16[2,1024,1024]{2,1,0:T(8,128)(2,1)} fusion(bf16[2,1024,1152]{1,2,0:T(8,128)(2,1)} %get-tuple-element.257, bf16[1024,3456]{0,1:T(8,128)(2,1)} %all-gather.11.cloned.1.call-done), kind=kOutput, calls=%fused_computation.97 | convolution fusion | flops 4833935360 | bytes 11272192 | tf_op jit(solution)/shard_map/yhp,np->yhn/dot_general | solution.py:61
  495.0 4.4 fusion.82
  501.8 96.6 %while.27 = (s32[]{:T(128)}, f32[2,1024,4,64]{1,3,2,0:T(8,128)}, f32[2,1024,2,64]{1,3,2,0:T(8,128)}, bf16[2,1024,2,64]{1,3,2,0:T(8,128)(2,1)}, bf16[2,1024,2,64]...) while((s32[]{:T(128)}, f32[2,1024,4,64]{1,3,2,0:T(8,128)}, ...), condition=%wide.region_17.18_spmd, body=%wide.region_15.17_spmd.sunk | while | flops 2750935040 | bytes 241103568 | solution.py:239
  504.9 8.1 fusion.157
  513.1 8.9 fusion.162
  522.0 13.6 %fusion.159 = (f32[2,2,1024]{2,1,0:T(2,128)}, f32[2,1024,1024,2]{2,1,3,0:T(8,128)}) fusion(f32[2,1024,1024,2]{2,1,3,0:T(8,128)} %fusion.157, f32[2,2,1024]{2,1,0:T(2,128)} %dynamic-slice_bitcast_fusion.6, pred[1024,1024]{0,1:T(8,128)(4,1)S(1)} %fusion.158, bf16[1024,2,2,64]{0,3,2,1:T(8,128)(2,1)} %bitcast.295, ...), kind=kOutput, calls=%fused_computation.24.clone.1 | convolution fusion | flops 557838336 | bytes 35422212 | tf_op jit(solution)/shard_map/while/body/eval_jaxpr/qkgd,tkd->kgqt/dot_general | solution.py:101
  535.7 8.4 fusion.160
  544.1 2.7 fusion.161
  552.9 8.1 fusion.157
  561.1 8.9 fusion.162
  570.0 13.6 %fusion.159 = (f32[2,2,1024]{2,1,0:T(2,128)}, f32[2,1024,1024,2]{2,1,3,0:T(8,128)}) fusion(f32[2,1024,1024,2]{2,1,3,0:T(8,128)} %fusion.157, f32[2,2,1024]{2,1,0:T(2,128)} %dynamic-slice_bitcast_fusion.6, pred[1024,1024]{0,1:T(8,128)(4,1)S(1)} %fusion.158, bf16[1024,2,2,64]{0,3,2,1:T(8,128)(2,1)} %bitcast.295, ...), kind=kOutput, calls=%fused_computation.24.clone.1 | convolution fusion | flops 557838336 | bytes 35422212 | tf_op jit(solution)/shard_map/while/body/eval_jaxpr/qkgd,tkd->kgqt/dot_general | solution.py:101
  583.7 8.4 fusion.160
  592.1 2.7 fusion.161
  602.3 2.7 multiply_add_fusion.1
  608.7 2.8 multiply_reduce_fusion
  613.2 5.1 bitcast_convert_fusion.2
  620.1 5.7 convolution_convert_fusion
  627.4 57.7 %reduce-scatter.19.cloned.1.call-done = bf16[128,768]{1,0:T(8,128)(2,1)} async-done(((bf16[1024,768]{1,0:T(8,128)(2,1)}), bf16[128,768]{1,0:T(8,128)(2,1)}) %reduce-scatter.19.cloned.1.call-update) | async-done | bytes 196624
  690.7 40.3 %reduce-scatter.15.cloned.1.call-done = bf16[2,256,1024]{2,1,0:T(8,128)(2,1)} async-done(((bf16[2,1024,1024]{2,1,0:T(8,128)(2,1)}), bf16[2,256,1024]{2,1,0:T(8,128)(2,1)}) %reduce-scatter.15.cloned.1.call-update) | async-done | bytes 1048592 | tf_op jit(solution)/shard_map/reduce_scatter | solution.py:254
  733.3 39.7 %psum.7 = f32[8,272]{1,0:T(8,128)S(1)} all-reduce(f32[8,272]{1,0:T(8,128)S(1)} %pad_maximum_fusion.13), channel_id=1, replica_groups=mesh['dp'=8,'tensor'=4] {'dp','tensor'}, use_global_device_ids=true, to_apply=%region_27.28 | all-reduce | flops 2176 | bytes 17408 | tf_op jit(solution)/shard_map/psum | solution.py:279
  774.2 4.7 reduce-scatter.13.cloned.1.call-done
  778.9 4.2 fusion.76
  783.1 128.9 %reduce-scatter.17.cloned.1.call-done = bf16[128,3456]{1,0:T(8,128)(2,1)} async-done(((bf16[1024,3456]{1,0:T(8,128)(2,1)}), bf16[128,3456]{1,0:T(8,128)(2,1)}) %reduce-scatter.17.cloned.1.call-update) | async-done | bytes 884752 | tf_op jit(solution)/shard_map/reduce_scatter | solution.py:234
  (319 shorter events, 67.6 us)
Async XLA Ops:
  7.2 56.5 %all-gather.9.cloned.1.call-start = ((), (), s32[]{:S(2)}) async-start(), calls=%async_computation.7 | async-start | bytes 2064384 | tf_op jit(solution)/shard_map/all_gather | solution.py:162
  12.9 85.0 %all-gather.7.cloned.1.call-start = ((), (), s32[]{:S(2)}) async-start(), calls=%async_computation.6 | async-start | bytes 5242880 | tf_op jit(solution)/shard_map/all_gather | solution.py:163
  13.7 172.4 %reduce-scatter.9.cloned.1.call-start = ((), (), s32[]{:S(2)}) async-start(), calls=%async_computation.8 | async-start | bytes 5242880 | tf_op jit(solution)/shard_map/reduce_scatter | solution.py:196
  16.5 91.6 %copy-start.18 = (f32[2,1024,32]{1,2,0:T(8,128)}, f32[2,1024,32]{1,2,0:T(8,128)S(1)}, u32[]{:S(2)}) copy-start(f32[2,1024,32]{1,2,0:T(8,128)S(1)} %get-tuple-element.280) | copy-start | bytes 786436
  16.5 91.6 %copy-start.19 = (f32[2,1024,32]{1,2,0:T(8,128)}, f32[2,1024,32]{1,2,0:T(8,128)S(1)}, u32[]{:S(2)}) copy-start(f32[2,1024,32]{1,2,0:T(8,128)S(1)} %get-tuple-element.281) | copy-start | bytes 786436
  65.0 40.5 %copy-start.53 = (f32[1024,1]{0,1:T(1,128)}, f32[1024,1]{0,1:T(1,128)S(1)}, u32[]{:S(2)}) copy-start(f32[1024,1]{0,1:T(1,128)S(1)} %get-tuple-element.275) | copy-start | bytes 12292
  65.1 41.3 %copy-start.63 = (f32[64]{0:T(128)}, f32[64]{0:T(128)S(1)}, u32[]{:S(2)}) copy-start(f32[64]{0:T(128)S(1)} %mul.490) | copy-start | bytes 772
  65.2 40.9 %copy-start.59 = (f32[64]{0:T(128)}, f32[64]{0:T(128)S(1)}, u32[]{:S(2)}) copy-start(f32[64]{0:T(128)S(1)} %mul.475) | copy-start | bytes 772
  141.4 44.7 %copy-start.6 = (bf16[2,256,1024]{2,1,0:T(8,128)(2,1)S(1)}, bf16[2,256,1024]{2,1,0:T(8,128)(2,1)}, u32[]{:S(2)}) copy-start(bf16[2,256,1024]{2,1,0:T(8,128)(2,1)} %param.18) | copy-start | bytes 3145732
  141.4 46.4 %copy-start.49 = (f32[1024,1]{0,1:T(1,128)S(1)}, f32[1024,1]{0,1:T(1,128)}, u32[]{:S(2)}) copy-start(f32[1024,1]{0,1:T(1,128)} %get-tuple-element.272) | copy-start | bytes 12292
  141.4 156.8 %all-gather.11.cloned.1.call-start = ((), (), s32[]{:S(2)}) async-start(), calls=%async_computation.9 | async-start | bytes 7962624 | tf_op jit(solution)/shard_map/all_gather | solution.py:172
  144.0 189.1 %all-gather.15.cloned.1.call-start = ((), (), s32[]{:S(2)}) async-start(), calls=%async_computation.11 | async-start | bytes 5242880 | tf_op jit(solution)/shard_map/all_gather | solution.py:203
  187.8 261.4 %copy-start.51 = (f32[2,256]{1,0:T(2,128)}, f32[2,256]{1,0:T(2,128)S(1)}, u32[]{:S(2)}) copy-start(f32[2,256]{1,0:T(2,128)S(1)} %fusion.95) | copy-start | bytes 6148
  190.4 178.7 %all-gather.13.cloned.1.call-start = ((), (), s32[]{:S(2)}) async-start(), calls=%async_computation.10 | async-start | bytes 5242880 | tf_op jit(solution)/shard_map/all_gather | solution.py:175
  191.0 255.2 %reduce-scatter.11.cloned.1.call-start = ((), (), s32[]{:S(2)}) async-start(), calls=%async_computation.12 | async-start | bytes 5242880 | tf_op jit(solution)/shard_map/reduce_scatter | solution.py:219
  401.5 44.7 %copy-start.10 = (bf16[2,256,1024]{2,1,0:T(8,128)(2,1)S(1)}, bf16[2,256,1024]{2,1,0:T(8,128)(2,1)}, u32[]{:S(2)}) copy-start(bf16[2,256,1024]{2,1,0:T(8,128)(2,1)} %reduce-scatter.9.cloned.1.call-done) | copy-start | bytes 3145732
  401.5 93.5 %all-gather.17.cloned.1.call-start = ((), (), s32[]{:S(2)}) async-start(), calls=%async_computation.13 | async-start | bytes 5242880 | tf_op jit(solution)/shard_map/all_gather | solution.py:232
  452.6 232.5 %reduce-scatter.19.cloned.1.call-start = ((), (), s32[]{:S(2)}) async-start(), calls=%async_computation.17 | async-start | bytes 1769472
  454.9 8.7 copy-start.65
  484.9 10.1 %copy-start.27 = (bf16[2,1024,256]{1,2,0:T(8,128)(2,1)S(1)}, bf16[2,1024,256]{1,2,0:T(8,128)(2,1)}, u32[]{:S(2)}) copy-start(bf16[2,1024,256]{1,2,0:T(8,128)(2,1)} %get-tuple-element.108) | copy-start | bytes 3145732
  504.9 8.2 copy-start.5
  504.9 8.2 copy-start.28
  513.1 22.6 %slice-start = ((s8[16777216]{0:T(1024)(128)(4,1)}), s8[4194304]{0:T(1024)(128)(4,1)S(1)}, s32[]{:S(2)}) async-start(s8[16777216]{0:T(1024)(128)(4,1)} %bitcast.288), calls=%async_computation.18 | async-start | bytes 8388608 | tf_op jit(solution)/shard_map/while
  513.1 22.6 %slice-start.1 = ((s8[16777216]{0:T(1024)(128)(4,1)}), s8[4194304]{0:T(1024)(128)(4,1)S(1)}, s32[]{:S(2)}) async-start(s8[16777216]{0:T(1024)(128)(4,1)} %bitcast.288), calls=%async_computation.19 | async-start | bytes 8388608 | tf_op jit(solution)/shard_map/while
  522.0 13.6 %slice-start.2 = ((s8[16777216]{0:T(1024)(128)(4,1)}), s8[4194304]{0:T(1024)(128)(4,1)S(1)}, s32[]{:S(2)}) async-start(s8[16777216]{0:T(1024)(128)(4,1)} %bitcast.288), calls=%async_computation.20 | async-start | bytes 8388608 | tf_op jit(solution)/shard_map/while
  522.0 13.6 %slice-start.3 = ((s8[16777216]{0:T(1024)(128)(4,1)}), s8[4194304]{0:T(1024)(128)(4,1)S(1)}, s32[]{:S(2)}) async-start(s8[16777216]{0:T(1024)(128)(4,1)} %bitcast.288), calls=%async_computation.21 | async-start | bytes 8388608 | tf_op jit(solution)/shard_map/while
  535.7 8.4 copy-start.1
  535.7 8.4 copy-start.32
  552.9 8.2 copy-start.5
  552.9 8.2 copy-start.28
  561.1 22.6 %slice-start = ((s8[16777216]{0:T(1024)(128)(4,1)}), s8[4194304]{0:T(1024)(128)(4,1)S(1)}, s32[]{:S(2)}) async-start(s8[16777216]{0:T(1024)(128)(4,1)} %bitcast.288), calls=%async_computation.18 | async-start | bytes 8388608 | tf_op jit(solution)/shard_map/while
  561.1 22.6 %slice-start.1 = ((s8[16777216]{0:T(1024)(128)(4,1)}), s8[4194304]{0:T(1024)(128)(4,1)S(1)}, s32[]{:S(2)}) async-start(s8[16777216]{0:T(1024)(128)(4,1)} %bitcast.288), calls=%async_computation.19 | async-start | bytes 8388608 | tf_op jit(solution)/shard_map/while
  570.0 13.6 %slice-start.2 = ((s8[16777216]{0:T(1024)(128)(4,1)}), s8[4194304]{0:T(1024)(128)(4,1)S(1)}, s32[]{:S(2)}) async-start(s8[16777216]{0:T(1024)(128)(4,1)} %bitcast.288), calls=%async_computation.20 | async-start | bytes 8388608 | tf_op jit(solution)/shard_map/while
  570.0 13.6 %slice-start.3 = ((s8[16777216]{0:T(1024)(128)(4,1)}), s8[4194304]{0:T(1024)(128)(4,1)S(1)}, s32[]{:S(2)}) async-start(s8[16777216]{0:T(1024)(128)(4,1)} %bitcast.288), calls=%async_computation.21 | async-start | bytes 8388608 | tf_op jit(solution)/shard_map/while
  583.6 8.4 copy-start.1
  583.7 8.4 copy-start.32
  598.4 6.6 slice-start.4
  598.4 6.6 copy-start.44
  620.1 111.0 %reduce-scatter.15.cloned.1.call-start = ((), (), s32[]{:S(2)}) async-start(), calls=%async_computation.15 | async-start | bytes 5242880 | tf_op jit(solution)/shard_map/reduce_scatter | solution.py:254
  625.8 153.1 %reduce-scatter.13.cloned.1.call-start = ((), (), s32[]{:S(2)}) async-start(), calls=%async_computation.14 | async-start | bytes 5242880 | tf_op jit(solution)/shard_map/reduce_scatter | solution.py:235
  626.6 104.5 %copy-start.7 = (bf16[2,256,1024]{2,1,0:T(8,128)(2,1)S(1)}, bf16[2,256,1024]{2,1,0:T(8,128)(2,1)}, u32[]{:S(2)}) copy-start(bf16[2,256,1024]{2,1,0:T(8,128)(2,1)} %param.18) | copy-start | bytes 3145732
  626.6 106.7 %copy-start.58 = (f32[1024]{0:T(1024)S(1)}, f32[1024]{0:T(1024)}, u32[]{:S(2)}) copy-start(f32[1024]{0:T(1024)} %get-tuple-element.208) | copy-start | bytes 12292
  626.6 152.3 %copy-start.11 = (bf16[2,256,1024]{2,1,0:T(8,128)(2,1)S(1)}, bf16[2,256,1024]{2,1,0:T(8,128)(2,1)}, u32[]{:S(2)}) copy-start(bf16[2,256,1024]{2,1,0:T(8,128)(2,1)} %reduce-scatter.9.cloned.1.call-done) | copy-start | bytes 3145732
  626.6 152.3 %copy-start.15 = (bf16[2,256,1024]{2,1,0:T(8,128)(2,1)S(1)}, bf16[2,256,1024]{2,1,0:T(8,128)(2,1)}, u32[]{:S(2)}) copy-start(bf16[2,256,1024]{2,1,0:T(8,128)(2,1)} %param.31) | copy-start | bytes 3145732
  626.6 152.3 %copy-start.50 = (f32[1024,1]{0,1:T(1,128)S(1)}, f32[1024,1]{0,1:T(1,128)}, u32[]{:S(2)}) copy-start(f32[1024,1]{0,1:T(1,128)} %get-tuple-element.272) | copy-start | bytes 12292
  626.6 152.3 %copy-start.52 = (f32[2,256]{1,0:T(2,128)S(1)}, f32[2,256]{1,0:T(2,128)}, u32[]{:S(2)}) copy-start(f32[2,256]{1,0:T(2,128)} %copy-done.51) | copy-start | bytes 6148
  626.6 152.3 %copy-start.56 = (f32[2,256]{1,0:T(2,128)S(1)}, f32[2,256]{1,0:T(2,128)}, u32[]{:S(2)}) copy-start(f32[2,256]{1,0:T(2,128)} %copy-done.55) | copy-start | bytes 6148
  626.6 285.3 %reduce-scatter.17.cloned.1.call-start = ((), (), s32[]{:S(2)}) async-start(), calls=%async_computation.16 | async-start | bytes 7962624 | tf_op jit(solution)/shard_map/reduce_scatter | solution.py:234
  (59 other events, 159.2 us)
Sparse Core Ops, SparseCore 0:
  13.0 50.5 all-gather.8
  65.2 32.6 all-gather.6
  141.5 44.5 reduce-scatter.8
  188.8 109.4 all-gather.10
  300.3 32.6 all-gather.14
  334.5 34.4 all-gather.12
  401.6 44.5 reduce-scatter.10
  452.7 34.4 all-gather.16
  620.2 64.8 reduce-scatter.18
  687.6 43.4 reduce-scatter.14
  733.6 45.2 reduce-scatter.12
  782.9 129.0 reduce-scatter.16

commit v2 on v1

--- a/solution.py
+++ b/solution.py
@@ -120,6 +120,13 @@
         * score_scale
     )
     return (query_grad.reshape(seq_len, heads, head_dim), key_grad, value_grad.astype(jnp.bfloat16))
+
+
+def each_sequence(attend, packed):
+    results = [
+        attend(tuple(part[index] for part in packed)) for index in range(packed[0].shape[0])
+    ]
+    return tuple(jnp.stack(parts) for parts in zip(*results))
 
 
 def on_device(
@@ -168,10 +175,10 @@
     ffn_gain = gains[:, 1]
     query_gain = gains[:, 2].reshape(parts, share)[:, :gain_share].reshape(-1)
     key_gain = gains[:, 3].reshape(parts, share)[:, :gain_share].reshape(-1)
-    ffn_pack = jnp.concatenate([w_gate, w_up, w_down.T], axis=1)
-    ffn_all = lax.all_gather(ffn_pack, "dp", axis=0, tiled=True)
-    gate_up_weight = ffn_all[:, : 2 * hidden_units]
-    down_weight_t = ffn_all[:, 2 * hidden_units :]
+    gate_up_weight = lax.all_gather(
+        jnp.concatenate([w_gate, w_up], axis=1), "dp", axis=0, tiled=True
+    )
+    down_weight_t = lax.all_gather(w_down.T, "dp", axis=0, tiled=True)
     grad_full = lax.all_gather(out_grad, "tensor", axis=1, tiled=True)
 
     inputs = tokens.astype(jnp.float32)
@@ -192,20 +199,19 @@
         .astype(jnp.bfloat16)
         .reshape(seq_count, seq_len, -1, head_dim)
     )
-    mixture, log_total = lax.map(attend_forward, (queries, key_rows, value_rows, doc_ids))
+    mixture, log_total = each_sequence(attend_forward, (queries, key_rows, value_rows, doc_ids))
+    attn_sums = project_back(mixture, out_weight_t).astype(jnp.bfloat16)
+    attn_sums, gate_up_weight = lax.optimization_barrier((attn_sums, gate_up_weight))
     attn_out = lax.psum_scatter(
-        project_back(mixture, out_weight_t).astype(jnp.bfloat16),
+        attn_sums,
         "tensor",
         scatter_dimension=1,
         tiled=True,
     ).astype(jnp.float32)
     mid_stream = inputs + attn_out
-    normed_mid = lax.all_gather(
-        rms_scale(mid_stream, ffn_gain).astype(jnp.bfloat16),
-        "tensor",
-        axis=1,
-        tiled=True,
-    )
+    normed_mine = rms_scale(mid_stream, ffn_gain).astype(jnp.bfloat16)
+    normed_mine, down_weight_t = lax.optimization_barrier((normed_mine, down_weight_t))
+    normed_mid = lax.all_gather(normed_mine, "tensor", axis=1, tiled=True)
     gate_up = project(normed_mid, gate_up_weight)
     gate_proj = gate_up[..., :hidden_units]
     up_proj = gate_up[..., hidden_units:]
@@ -230,13 +236,12 @@
     stream_grad, ffn_gain_grad = mid_pull(mid_norm_grad)
     mid_grad = out_grad.astype(jnp.float32) + stream_grad
     mid_low = lax.all_gather(mid_grad.astype(jnp.bfloat16), "tensor", axis=1, tiled=True)
-    mid_low, ffn_w_grads, ffn_sums = lax.optimization_barrier((mid_low, ffn_w_grads, ffn_sums))
+    mid_low, ffn_w_grads = lax.optimization_barrier((mid_low, ffn_w_grads))
     ffn_summed = lax.psum_scatter(ffn_w_grads, "dp", scatter_dimension=0, tiled=True)
     ffn_out = lax.psum_scatter(ffn_sums, "tensor", scatter_dimension=1, tiled=True)
-    block_out = (mid_stream + ffn_out.astype(jnp.float32)).astype(jnp.bfloat16)
     out_w_grad_t = weight_grad(mid_low, mixture)
     mix_grad = project(mid_low, out_weight_t).astype(jnp.bfloat16)
-    query_grad, key_grad, value_grad = lax.map(
+    query_grad, key_grad, value_grad = each_sequence(
         attend_backward, (queries, key_rows, value_rows, doc_ids, log_total, mix_grad)
     )
     query_pull = jax.vjp(query_side, query_raw, query_gain)[1]
@@ -251,14 +256,20 @@
         ],
         axis=-1,
     )
+    qkv_low, ffn_summed, ffn_out = lax.optimization_barrier((qkv_low, ffn_summed, ffn_out))
+    block_out = (mid_stream + ffn_out.astype(jnp.float32)).astype(jnp.bfloat16)
+    input_sums = project_back(qkv_low, qkv_weight)
+    attn_gain_grad = jnp.sum(
+        input_sums * rms_scale(tokens_full.astype(jnp.float32), 1.0), axis=(0, 1)
+    )
     input_norm_grad = lax.psum_scatter(
-        project_back(qkv_low, qkv_weight).astype(jnp.bfloat16),
+        input_sums.astype(jnp.bfloat16),
         "tensor",
         scatter_dimension=1,
         tiled=True,
     ).astype(jnp.float32)
     input_pull = jax.vjp(rms_scale, inputs, attn_gain)[1]
-    input_grad, attn_gain_grad = input_pull(input_norm_grad)
+    input_grad = input_pull(input_norm_grad)[0]
     tokens_grad = mid_grad + input_grad
     gain_cut = jnp.concatenate(
         [

time: 928 us -> 787 us (0.85)
  waiting for transfers between devices: 562 us -> 415 us
  other arithmetic: 70.9 us -> 86 us
    reduce_scatter x1, waiting for transfers between devices: 129 us -> 73 us  [on_device(): lax.psum_scatter(ffn_w_grads, 'dp', scatter_dimension=0, tiled=True)]
    unnamed x13 -> x14, waiting for transfers between devices: 60.2 us -> 10.8 us
    all_gather x2 -> x3, waiting for transfers between devices: 142 us -> 106 us  [the longest x1 51.6 us: on_device(): down_weight_t = lax.all_gather(w_down.T, 'dp', axis=0, tiled=True)]
    dot_general x4 -> x2, matrix products: 22.4 us -> 15.3 us  [score_block(): jnp.einsum('qkgd,tkd->kgqt', grouped, key_rows, preferred_element_type=jn...]
    unnamed x117 -> x173, local copies, waits for them, and re-layouts: 17 us -> 21.3 us
  transfers between devices with their start and end apart: 12 -> 13, of which waited for: 11 -> 11; matrix products, arithmetic and copies ran while one was open for 9% -> 31% of each run, Pallas kernels for 0% -> 0%
where the time goes in v2:
time: 787 us; the launch traced here: 780 us
  waiting for transfers between devices  415 us (53%)
  matrix products  189 us (24%)
  other arithmetic  86 us (11%)
  blocking collectives  39.6 us (5%)
  local copies, waits for them, and re-layouts  34.5 us (4%)
  between operations  15.4 us (2%)
    reduce_scatter x1, waiting for transfers between devices, on_device(): lax.psum_scatter(ffn_w_grads, 'dp', scatter_dimension=0, tiled=True)  73 us
    all_gather x1, waiting for transfers between devices, on_device(): down_weight_t = lax.all_gather(w_down.T, 'dp', axis=0, tiled=True)  51.6 us
    reduce_scatter x1, waiting for transfers between devices, on_device(): lax.psum_scatter(project_back(gate_up_grad, gate_up_weight).astype(jnp.bf...  44.6 us
    reduce_scatter x1, waiting for transfers between devices, on_device(): lax.psum_scatter(attn_sums, 'tensor', scatter_dimension=1, tiled=True)  44.4 us
    all_gather x1, waiting for transfers between devices, on_device(): attn_all = lax.all_gather(attn_pack, 'dp', axis=0, tiled=True)  43 us
    reduce_scatter x1, waiting for transfers between devices, on_device(): lax.psum_scatter(input_sums.astype(jnp.bfloat16), 'tensor', scatter_dimen...  40.5 us
    psum x1, blocking collectives, on_device(): lax.psum(gain_cut, ('dp', 'tensor'))  39.6 us
    dot_general x4, matrix products, project(): jnp.einsum('xpo,oh->xph', matmul_operand, weight_matrix, preferred_elemen...  38.7 us
  transfers between devices with their start and end apart: 13, of which 11 were waited for; matrix products, arithmetic and copies ran while one was open for 31% of the time, Pallas kernels for 0%

profile of v2, /device:TPU:0, one launch (start us, length us, event | category | flops | bytes accessed | tf_op | source)
XLA Modules:
  0.0 780.0 jit_solution(8975514687018151935)
XLA Ops:
  20.6 43.0 %all-gather.10.cloned.1.call-done = bf16[1024,896]{0,1:T(8,128)(2,1)} async-done(((bf16[128,896]{0,1:T(8,128)(2,1)}), bf16[1024,896]{0,1:T(8,128)(2,1)}) %all-gather.10.cloned.1.call-update) | async-done | bytes 1835024 | tf_op jit(solution)/shard_map/all_gather | solution.py:169
  64.6 33.4 %all-gather.8.cloned.1.call-done = bf16[2,1024,1024]{2,1,0:T(8,128)(2,1)} async-done(((bf16[2,256,1024]{2,1,0:T(8,128)(2,1)}), bf16[2,1024,1024]{2,1,0:T(8,128)(2,1)}) %all-gather.8.cloned.1.call-update) | async-done | bytes 4194320 | tf_op jit(solution)/shard_map/all_gather | solution.py:170
  98.0 3.2 fusion.19
  101.4 3.7 fusion.112
  108.8 7.7 fusion.113
  116.5 8.1 %fusion.7 = f32[2,2,1024]{2,1,0:T(2,128)S(1)} fusion(f32[2,2,1024,1024]{2,3,1,0:T(8,128)} %get-tuple-element.119, f32[2,2,1024]{2,1,0:T(2,128)S(1)} %get-tuple-element.118), kind=kLoop, calls=%fused_computation.19 | loop fusion | flops 8384512 | bytes 16809984 | tf_op jit(solution)/shard_map/reduce_sum | solution.py:88
  124.6 7.4 fusion.57
  132.3 7.6 fusion.114
  139.9 8.0 %fusion.6 = f32[2,2,1024]{2,1,0:T(2,128)S(1)} fusion(f32[2,2,1024,1024]{2,3,1,0:T(8,128)} %get-tuple-element.121, f32[2,2,1024]{2,1,0:T(2,128)S(1)} %get-tuple-element.120), kind=kLoop, calls=%fused_computation.18 | loop fusion | flops 8384512 | bytes 16809984 | tf_op jit(solution)/shard_map/reduce_sum | solution.py:88
  147.9 7.9 %fusion.58 = bf16[2,64,2,1024]{3,1,2,0:T(8,128)(2,1)S(1)} fusion(bf16[1024,2,64,1]{0,2,3,1:T(8,128)(2,1)S(1)} %bitcast.246, f32[2,2,1024,1024]{2,3,1,0:T(8,128)} %get-tuple-element.121, f32[2,2,1024]{2,1,0:T(2,128)S(1)} %fusion.6, f32[2,2,1024]{2,1,0:T(2,128)S(1)} %get-tuple-element.120), kind=kOutput, calls=%fused_computation.104 | convolution fusion | flops 549715968 | bytes 17596416 | tf_op jit(solution)/shard_map/kgqt,tkd->qkgd/dot_general | solution.py:90
  156.1 4.5 convolution_convert_fusion.1
  160.5 20.1 %all-gather.12.cloned.1.call-done = bf16[1024,2304]{1,0:T(8,128)(2,1)} async-done(((bf16[128,2304]{1,0:T(8,128)(2,1)}), bf16[1024,2304]{1,0:T(8,128)(2,1)}) %all-gather.12.cloned.1.call-update) | async-done | bytes 4718608 | tf_op jit(solution)/shard_map/all_gather | solution.py:178
  181.3 44.4 %reduce-scatter.9.cloned.1.call-done = bf16[2,256,1024]{2,1,0:T(8,128)(2,1)} async-done(((bf16[2,1024,1024]{2,1,0:T(8,128)(2,1)}), bf16[2,256,1024]{2,1,0:T(8,128)(2,1)}) %reduce-scatter.9.cloned.1.call-update) | async-done | bytes 1048592 | tf_op jit(solution)/shard_map/reduce_scatter | solution.py:205
  227.3 2.6 multiply_convert_fusion.1
  229.9 51.6 %all-gather.14.cloned.1.call-done = bf16[1024,1152]{0,1:T(8,128)(2,1)} async-done(((bf16[128,1152]{0,1:T(8,128)(2,1)}), bf16[1024,1152]{0,1:T(8,128)(2,1)}) %all-gather.14.cloned.1.call-update) | async-done | bytes 2359312 | tf_op jit(solution)/shard_map/all_gather | solution.py:181
  282.4 33.9 %all-gather.18.cloned.1.call-done = bf16[2,1024,1024]{2,1,0:T(8,128)(2,1)} async-done(((bf16[2,256,1024]{2,1,0:T(8,128)(2,1)}), bf16[2,1024,1024]{2,1,0:T(8,128)(2,1)}) %all-gather.18.cloned.1.call-update) | async-done | bytes 4194320 | tf_op jit(solution)/shard_map/all_gather | solution.py:214
  316.3 16.8 %fusion.30 = f32[2,1024,2304]{1,2,0:T(8,128)} fusion(bf16[2,1024,1024]{2,1,0:T(8,128)(2,1)} %all-gather.18.cloned.1.call-done, bf16[1024,2304]{1,0:T(8,128)(2,1)} %all-gather.12.cloned.1.call-done), kind=kOutput, calls=%fused_computation.51 | convolution fusion | flops 9663676416 | bytes 27787264 | tf_op jit(solution)/shard_map/xpo,oh->xph/dot_general | solution.py:55
  333.2 19.3 %all-gather.16.cloned.1.call-done = bf16[2,1024,1024]{2,1,0:T(8,128)(2,1)} async-done(((bf16[2,256,1024]{2,1,0:T(8,128)(2,1)}), bf16[2,1024,1024]{2,1,0:T(8,128)(2,1)}) %all-gather.16.cloned.1.call-update) | async-done | bytes 4194320 | tf_op jit(solution)/shard_map/all_gather | solution.py:182
  352.5 15.7 %fusion.14 = (bf16[2,1024,1152]{1,2,0:T(8,128)(2,1)S(1)}, bf16[2,1024,1152]{1,2,0:T(8,128)(2,1)}, bf16[2,1024,1152]{1,2,0:T(8,128)(2,1)}) fusion(f32[2,1024,2304]{1,2,0:T(8,128)} %fusion.30, bf16[2,1024,1024]{2,1,0:T(8,128)(2,1)} %all-gather.16.cloned.1.call-done, bf16[1024,1152]{0,1:T(8,128)(2,1)S(1)} %copy-done.70), kind=kOutput, calls=%fused_computation.29 | convolution fusion | flops 4869586944 | bytes 39583744 | tf_op jit(solution)/shard_map/xpo,oh->xph/dot_general | solution.py:55
  368.2 2.1 copy-done.71
  370.3 14.9 %fusion.39 = bf16[2,1024,1024]{2,1,0:T(8,128)(2,1)} fusion(bf16[1024,2304]{1,0:T(8,128)(2,1)} %all-gather.12.cloned.1.call-done, bf16[2,1024,1152]{1,2,0:T(8,128)(2,1)} %get-tuple-element.78, bf16[2,1024,1152]{1,2,0:T(8,128)(2,1)S(1)} %get-tuple-element.77), kind=kOutput, calls=%fused_computation.66 | convolution fusion | flops 9684647936 | bytes 18350080 | tf_op jit(solution)/shard_map/yhp,np->yhn/dot_general | solution.py:61
  385.3 44.6 %reduce-scatter.11.cloned.1.call-done = bf16[2,256,1024]{2,1,0:T(8,128)(2,1)} async-done(((bf16[2,1024,1024]{2,1,0:T(8,128)(2,1)}), bf16[2,256,1024]{2,1,0:T(8,128)(2,1)}) %reduce-scatter.11.cloned.1.call-update) | async-done | bytes 1048592 | tf_op jit(solution)/shard_map/reduce_scatter | solution.py:225
  429.9 3.0 fusion.48
  432.9 3.0 fusion.78
  436.0 9.6 %convolution_convert_fusion = bf16[2,1024,1024]{2,1,0:T(8,128)(2,1)} fusion(bf16[2,1024,1152]{1,2,0:T(8,128)(2,1)} %get-tuple-element.79, bf16[1024,1152]{0,1:T(8,128)(2,1)} %all-gather.14.cloned.1.call-done), kind=kOutput, calls=%fused_computation.67 | convolution fusion | flops 4833935360 | bytes 11272192 | tf_op jit(solution)/shard_map/yhp,np->yhn/dot_general | solution.py:61
  445.7 10.3 %fusion.34 = bf16[1024,1152]{1,0:T(8,128)(2,1)} fusion(bf16[2,1024,1152]{1,2,0:T(8,128)(2,1)} %get-tuple-element.79, bf16[2,1024,1024]{2,1,0:T(8,128)(2,1)} %all-gather.16.cloned.1.call-done), kind=kOutput, calls=%fused_computation.60 | convolution fusion | flops 4833017856 | bytes 11272192 | tf_op jit(solution)/shard_map/wba,wbh->ah/dot_general | solution.py:67
  456.0 14.2 %bitcast_convert_fusion = bf16[1024,2304]{1,0:T(8,128)(2,1)S(1)} fusion(bf16[2,1024,1024]{2,1,0:T(8,128)(2,1)S(1)} %copy-done.69, bf16[2,1024,1152]{1,2,0:T(8,128)(2,1)} %get-tuple-element.78, bf16[2,1024,1152]{1,2,0:T(8,128)(2,1)} %copy-done.71), kind=kOutput, calls=%fused_computation.31 | convolution fusion | flops 9684910080 | bytes 18350080 | tf_op jit(solution)/shard_map/wba,wbh->ah/dot_general | solution.py:67
  470.2 5.0 pad_maximum_fusion.1
  475.3 2.5 slice.187
  477.8 3.5 slice.193
  481.4 2.5 convolution_convert_fusion.2
  484.0 15.5 %fusion = (f32[2,2,1024]{2,1,0:T(2,128)S(1)}, f32[2,1024,1024,2]{2,1,3,0:T(8,128)}) fusion(f32[2,2,1024,1024]{2,3,1,0:T(8,128)} %get-tuple-element.119, f32[2,2,1024]{2,1,0:T(2,128)S(1)} %log_add_fusion, bf16[1024,2,64,1]{0,2,3,1:T(8,128)(2,1)S(1)} %bitcast.249, bf16[1024,2,2,64]{0,3,2,1:T(8,128)(2,1)S(1)} %bitcast.233), kind=kOutput, calls=%fused_computation.2 | convolution fusion | flops 549449728 | bytes 34373632 | tf_op jit(solution)/shard_map/qkgd,tkd->kgqt/dot_general | solution.py:101
  501.1 8.4 %fusion.2 = bf16[2,2,1024,1024]{2,3,1,0:T(8,128)(2,1)S(1)} fusion(f32[2,1024,1024,2]{2,1,3,0:T(8,128)} %get-tuple-element.123, f32[2,2,1024,1024]{2,3,1,0:T(8,128)S(1)} %bitcast.225, f32[2,2,1024]{2,1,0:T(2,128)S(1)} %get-tuple-element.122, f32[2,2,1024]{2,1,0:T(2,128)S(1)} %log_add_fusion), kind=kLoop, calls=%fused_computation.4 | loop fusion | flops 16777216 | bytes 41975808 | tf_op jit(solution)/shard_map/convert_element_type | solution.py:110
  509.5 3.5 fusion.68
  513.0 10.8 %fusion.3 = (f32[2,2,1024]{2,1,0:T(2,128)S(1)}, f32[2,1024,1024,2]{2,1,3,0:T(8,128)}) fusion(f32[2,2,1024,1024]{2,3,1,0:T(8,128)} %get-tuple-element.121, f32[2,2,1024]{2,1,0:T(2,128)S(1)} %log_add_fusion.1, bf16[1024,2,64,1]{0,2,3,1:T(8,128)(2,1)S(1)} %bitcast.247, bf16[1024,2,2,64]{0,3,2,1:T(8,128)(2,1)S(1)} %bitcast.231), kind=kOutput, calls=%fused_computation.7 | convolution fusion | flops 549449728 | bytes 34373632 | tf_op jit(solution)/shard_map/qkgd,tkd->kgqt/dot_general | solution.py:101
  523.8 17.3 %fusion.5 = bf16[2,2,1024,1024]{2,3,1,0:T(8,128)(2,1)} fusion(f32[2,1024,1024,2]{2,1,3,0:T(8,128)} %get-tuple-element.125, f32[2,2,1024,1024]{2,3,1,0:T(8,128)} %get-tuple-element.121, f32[2,2,1024]{2,1,0:T(2,128)S(1)} %get-tuple-element.124, f32[2,2,1024]{2,1,0:T(2,128)S(1)} %log_add_fusion.1), kind=kLoop, calls=%fused_computation.9 | loop fusion | flops 16777216 | bytes 41975808 | tf_op jit(solution)/shard_map/convert_element_type | solution.py:110
  541.1 7.1 fusion.66
  550.0 2.4 multiply_reduce_fusion.4
  562.2 4.1 fusion.69
  566.4 8.7 %fusion.72 = bf16[2,64,1024]{2,1,0:T(8,128)(2,1)S(1)} fusion(bf16[1024,2,2,64]{0,3,2,1:T(8,128)(2,1)S(1)} %bitcast.232, f32[2,2,1024,1024]{2,3,1,0:T(8,128)} %get-tuple-element.121, f32[2,2,1024]{2,1,0:T(2,128)S(1)} %log_add_fusion.1), kind=kOutput, calls=%fused_computation.114 | convolution fusion | flops 545390592 | bytes 17580032 | tf_op jit(solution)/shard_map/kgqt,qkgd->tkd/dot_general | solution.py:104
  577.7 73.0 %reduce-scatter.13.cloned.1.call-done = bf16[128,3456]{1,0:T(8,128)(2,1)} async-done(((bf16[1024,3456]{1,0:T(8,128)(2,1)}), bf16[128,3456]{1,0:T(8,128)(2,1)}) %reduce-scatter.13.cloned.1.call-update) | async-done | bytes 884752 | tf_op jit(solution)/shard_map/reduce_scatter | solution.py:240
  650.7 4.6 bitcast_convert_fusion.2
  657.3 7.6 fusion.18
  667.1 2.3 copy.113
  669.5 39.6 %psum.7 = f32[8,272]{1,0:T(8,128)S(1)} all-reduce(f32[8,272]{1,0:T(8,128)S(1)} %pad_maximum_fusion.15), channel_id=1, replica_groups=mesh['dp'=8,'tensor'=4] {'dp','tensor'}, use_global_device_ids=true, to_apply=%region_27.28 | all-reduce | flops 2176 | bytes 17408 | tf_op jit(solution)/shard_map/psum | solution.py:290
  712.4 8.8 %reduce-scatter.19.cloned.1.call-done = bf16[128,768]{1,0:T(8,128)(2,1)} async-done(((bf16[1024,768]{1,0:T(8,128)(2,1)}), bf16[128,768]{1,0:T(8,128)(2,1)}) %reduce-scatter.19.cloned.1.call-update) | async-done | bytes 196624
  726.8 40.5 %reduce-scatter.17.cloned.1.call-done = bf16[2,256,1024]{2,1,0:T(8,128)(2,1)} async-done(((bf16[2,1024,1024]{2,1,0:T(8,128)(2,1)}), bf16[2,256,1024]{2,1,0:T(8,128)(2,1)}) %reduce-scatter.17.cloned.1.call-update) | async-done | bytes 1048592 | tf_op jit(solution)/shard_map/reduce_scatter | solution.py:265
  769.0 4.2 fusion.51
  (264 shorter events, 52.1 us)
Async XLA Ops:
  7.2 56.5 %all-gather.10.cloned.1.call-start = ((), (), s32[]{:S(2)}) async-start(), calls=%async_computation.7 | async-start | bytes 2064384 | tf_op jit(solution)/shard_map/all_gather | solution.py:169
  12.9 85.0 %all-gather.8.cloned.1.call-start = ((), (), s32[]{:S(2)}) async-start(), calls=%async_computation.6 | async-start | bytes 5242880 | tf_op jit(solution)/shard_map/all_gather | solution.py:170
  13.7 167.0 %all-gather.12.cloned.1.call-start = ((), (), s32[]{:S(2)}) async-start(), calls=%async_computation.8 | async-start | bytes 5308416 | tf_op jit(solution)/shard_map/all_gather | solution.py:178
  15.6 210.1 %reduce-scatter.9.cloned.1.call-start = ((), (), s32[]{:S(2)}) async-start(), calls=%async_computation.9 | async-start | bytes 5242880 | tf_op jit(solution)/shard_map/reduce_scatter | solution.py:205
  20.6 87.3 %copy-start.10 = (f32[2,1024,32]{1,2,0:T(8,128)}, f32[2,1024,32]{1,2,0:T(8,128)S(1)}, u32[]{:S(2)}) copy-start(f32[2,1024,32]{1,2,0:T(8,128)S(1)} %get-tuple-element.110) | copy-start | bytes 786436
  20.6 87.3 %copy-start.12 = (f32[2,1024,32]{1,2,0:T(8,128)}, f32[2,1024,32]{1,2,0:T(8,128)S(1)}, u32[]{:S(2)}) copy-start(f32[2,1024,32]{1,2,0:T(8,128)S(1)} %get-tuple-element.111) | copy-start | bytes 786436
  64.4 40.7 %copy-start.53 = (f32[1024,1]{0,1:T(1,128)}, f32[1024,1]{0,1:T(1,128)S(1)}, u32[]{:S(2)}) copy-start(f32[1024,1]{0,1:T(1,128)S(1)} %get-tuple-element.105) | copy-start | bytes 12292
  64.5 41.2 %copy-start.63 = (f32[64]{0:T(128)}, f32[64]{0:T(128)S(1)}, u32[]{:S(2)}) copy-start(f32[64]{0:T(128)S(1)} %mul.509) | copy-start | bytes 772
  64.6 41.6 %copy-start.58 = (f32[64]{0:T(128)}, f32[64]{0:T(128)S(1)}, u32[]{:S(2)}) copy-start(f32[64]{0:T(128)S(1)} %mul.494) | copy-start | bytes 772
  105.6 19.0 %copy-start.36 = (bf16[1,1024,128]{1,2,0:T(8,128)(2,1)}, bf16[1,1024,128]{1,2,0:T(8,128)(2,1)S(1)}, u32[]{:S(2)}) copy-start(bf16[1,1024,128]{1,2,0:T(8,128)(2,1)S(1)} %get-tuple-element.89) | copy-start | bytes 786436
  105.6 42.3 %copy-start.34 = (bf16[1,1024,128]{1,2,0:T(8,128)(2,1)}, bf16[1,1024,128]{1,2,0:T(8,128)(2,1)S(1)}, u32[]{:S(2)}) copy-start(bf16[1,1024,128]{1,2,0:T(8,128)(2,1)S(1)} %get-tuple-element.88) | copy-start | bytes 786436
  108.0 24.2 %copy-start.25 = (bf16[1,1024,4,64]{1,3,2,0:T(8,128)(2,1)}, bf16[1,1024,4,64]{1,3,2,0:T(8,128)(2,1)S(1)}, u32[]{:S(2)}) copy-start(bf16[1,1024,4,64]{1,3,2,0:T(8,128)(2,1)S(1)} %get-tuple-element.96) | copy-start | bytes 1572868
  108.2 24.1 %copy-start.20 = (bf16[2,1024,2,32]{1,3,2,0:T(8,128)(2,1)}, bf16[2,1024,2,32]{1,3,2,0:T(8,128)(2,1)S(1)}, u32[]{:S(2)}) copy-start(bf16[2,1024,2,32]{1,3,2,0:T(8,128)(2,1)S(1)} %get-tuple-element.92) | copy-start | bytes 786436
  108.2 24.1 %copy-start.22 = (bf16[2,1024,2,32]{1,3,2,0:T(8,128)(2,1)}, bf16[2,1024,2,32]{1,3,2,0:T(8,128)(2,1)S(1)}, u32[]{:S(2)}) copy-start(bf16[2,1024,2,32]{1,3,2,0:T(8,128)(2,1)S(1)} %get-tuple-element.93) | copy-start | bytes 786436
  132.2 23.8 %copy-start.29 = (bf16[1,1024,256]{2,1,0:T(8,128)(2,1)}, bf16[1,1024,256]{2,1,0:T(8,128)(2,1)S(1)}, u32[]{:S(2)}) copy-start(bf16[1,1024,256]{2,1,0:T(8,128)(2,1)S(1)} %copy.91) | copy-start | bytes 1572868
  156.0 24.6 %copy-start.31 = (bf16[1,1024,256]{2,1,0:T(8,128)(2,1)}, bf16[1,1024,256]{2,1,0:T(8,128)(2,1)S(1)}, u32[]{:S(2)}) copy-start(bf16[1,1024,256]{2,1,0:T(8,128)(2,1)S(1)} %copy.90) | copy-start | bytes 1572868
  156.0 69.7 %copy-start.3 = (bf16[2,256,1024]{2,1,0:T(8,128)(2,1)S(1)}, bf16[2,256,1024]{2,1,0:T(8,128)(2,1)}, u32[]{:S(2)}) copy-start(bf16[2,256,1024]{2,1,0:T(8,128)(2,1)} %param.14) | copy-start | bytes 3145732
  180.7 100.9 %all-gather.14.cloned.1.call-start = ((), (), s32[]{:S(2)}) async-start(), calls=%async_computation.10 | async-start | bytes 2654208 | tf_op jit(solution)/shard_map/all_gather | solution.py:181
  181.2 135.1 %all-gather.18.cloned.1.call-start = ((), (), s32[]{:S(2)}) async-start(), calls=%async_computation.12 | async-start | bytes 5242880 | tf_op jit(solution)/shard_map/all_gather | solution.py:214
  281.6 70.9 %all-gather.16.cloned.1.call-start = ((), (), s32[]{:S(2)}) async-start(), calls=%async_computation.11 | async-start | bytes 5242880 | tf_op jit(solution)/shard_map/all_gather | solution.py:182
  282.3 70.2 %copy-start.70 = (bf16[1024,1152]{0,1:T(8,128)(2,1)S(1)}, bf16[1024,1152]{0,1:T(8,128)(2,1)}, u32[]{:S(2)}) copy-start(bf16[1024,1152]{0,1:T(8,128)(2,1)} %all-gather.14.cloned.1.call-done) | copy-start | bytes 7077892
  282.3 147.6 %reduce-scatter.11.cloned.1.call-start = ((), (), s32[]{:S(2)}) async-start(), calls=%async_computation.13 | async-start | bytes 5242880 | tf_op jit(solution)/shard_map/reduce_scatter | solution.py:225
  385.2 44.7 %copy-start.5 = (bf16[2,256,1024]{2,1,0:T(8,128)(2,1)S(1)}, bf16[2,256,1024]{2,1,0:T(8,128)(2,1)}, u32[]{:S(2)}) copy-start(bf16[2,256,1024]{2,1,0:T(8,128)(2,1)} %reduce-scatter.9.cloned.1.call-done) | copy-start | bytes 3145732
  385.2 47.7 %copy-start.7 = (bf16[2,256,1024]{2,1,0:T(8,128)(2,1)S(1)}, bf16[2,256,1024]{2,1,0:T(8,128)(2,1)}, u32[]{:S(2)}) copy-start(bf16[2,256,1024]{2,1,0:T(8,128)(2,1)} %param.27) | copy-start | bytes 3145732
  385.2 90.0 %all-gather.20.cloned.1.call-start = ((), (), s32[]{:S(2)}) async-start(), calls=%async_computation.14 | async-start | bytes 5242880 | tf_op jit(solution)/shard_map/all_gather | solution.py:238
  432.9 12.6 %copy-start.55 = (f32[2,256]{1,0:T(2,128)}, f32[2,256]{1,0:T(2,128)S(1)}, u32[]{:S(2)}) copy-start(f32[2,256]{1,0:T(2,128)S(1)} %multiply_multiply_fusion.5) | copy-start | bytes 6148
  436.0 141.7 %reduce-scatter.15.cloned.1.call-start = ((), (), s32[]{:S(2)}) async-start(), calls=%async_computation.16 | async-start | bytes 5242880 | tf_op jit(solution)/shard_map/reduce_scatter | solution.py:241
  445.6 205.1 %reduce-scatter.13.cloned.1.call-start = ((), (), s32[]{:S(2)}) async-start(), calls=%async_computation.15 | async-start | bytes 7962624 | tf_op jit(solution)/shard_map/reduce_scatter | solution.py:240
  445.7 10.3 %copy-start.69 = (bf16[2,1024,1024]{2,1,0:T(8,128)(2,1)S(1)}, bf16[2,1024,1024]{2,1,0:T(8,128)(2,1)}, u32[]{:S(2)}) copy-start(bf16[2,1024,1024]{2,1,0:T(8,128)(2,1)} %all-gather.18.cloned.1.call-done) | copy-start | bytes 12582916
  475.3 245.9 %reduce-scatter.19.cloned.1.call-start = ((), (), s32[]{:S(2)}) async-start(), calls=%async_computation.18 | async-start | bytes 1769472
  483.9 15.5 %copy-start.17 = (bf16[1,1024,256]{1,2,0:T(8,128)(2,1)}, bf16[1,1024,256]{1,2,0:T(8,128)(2,1)S(1)}, u32[]{:S(2)}) copy-start(bf16[1,1024,256]{1,2,0:T(8,128)(2,1)S(1)} %get-tuple-element.95) | copy-start | bytes 1572868
  483.9 29.1 %copy-start.15 = (bf16[1,1024,256]{1,2,0:T(8,128)(2,1)}, bf16[1,1024,256]{1,2,0:T(8,128)(2,1)S(1)}, u32[]{:S(2)}) copy-start(bf16[1,1024,256]{1,2,0:T(8,128)(2,1)S(1)} %get-tuple-element.94) | copy-start | bytes 1572868
  483.9 15.5 %slice-start = ((s8[16777216]{0:T(1024)(128)(4,1)}), s8[4194304]{0:T(1024)(128)(4,1)S(1)}, s32[]{:S(2)}) async-start(s8[16777216]{0:T(1024)(128)(4,1)} %bitcast.224), calls=%async_computation.19 | async-start | bytes 8388608
  484.0 15.5 %slice-start.1 = ((s8[16777216]{0:T(1024)(128)(4,1)}), s8[4194304]{0:T(1024)(128)(4,1)S(1)}, s32[]{:S(2)}) async-start(s8[16777216]{0:T(1024)(128)(4,1)} %bitcast.224), calls=%async_computation.20 | async-start | bytes 8388608
  484.0 15.5 %slice-start.2 = ((s8[16777216]{0:T(1024)(128)(4,1)}), s8[4194304]{0:T(1024)(128)(4,1)S(1)}, s32[]{:S(2)}) async-start(s8[16777216]{0:T(1024)(128)(4,1)} %bitcast.224), calls=%async_computation.21 | async-start | bytes 8388608
  484.0 17.1 %slice-start.3 = ((s8[16777216]{0:T(1024)(128)(4,1)}), s8[4194304]{0:T(1024)(128)(4,1)S(1)}, s32[]{:S(2)}) async-start(s8[16777216]{0:T(1024)(128)(4,1)} %bitcast.224), calls=%async_computation.22 | async-start | bytes 8388608
  523.8 28.7 %slice-start.4 = ((s8[8388608]{0:T(1024)(128)(4,1)}), s8[4194304]{0:T(1024)(128)(4,1)S(1)}, s32[]{:S(2)}) async-start(s8[8388608]{0:T(1024)(128)(4,1)} %bitcast.226), calls=%async_computation.23 | async-start | bytes 8388608
  523.8 17.3 %copy-start.26 = (bf16[1,1024,4,64]{1,3,2,0:T(8,128)(2,1)S(1)}, bf16[1,1024,4,64]{1,3,2,0:T(8,128)(2,1)}, u32[]{:S(2)}) copy-start(bf16[1,1024,4,64]{1,3,2,0:T(8,128)(2,1)} %copy-done.25) | copy-start | bytes 1572868
  523.8 28.7 %slice-start.5 = ((s8[8388608]{0:T(1024)(128)(4,1)}), s8[4194304]{0:T(1024)(128)(4,1)S(1)}, s32[]{:S(2)}) async-start(s8[8388608]{0:T(1024)(128)(4,1)} %bitcast.226), calls=%async_computation.24 | async-start | bytes 8388608
  576.3 74.4 %copy-start.24 = (bf16[2,1024,512]{1,2,0:T(8,128)(2,1)}, bf16[2,1024,512]{1,2,0:T(8,128)(2,1)S(1)}, u32[]{:S(2)}) copy-start(bf16[2,1024,512]{1,2,0:T(8,128)(2,1)S(1)} %maximum_maximum_fusion) | copy-start | bytes 6291460
  576.3 74.4 %copy-start.54 = (f32[1024,1]{0,1:T(1,128)S(1)}, f32[1024,1]{0,1:T(1,128)}, u32[]{:S(2)}) copy-start(f32[1024,1]{0,1:T(1,128)} %copy-done.53) | copy-start | bytes 12292
  576.3 74.4 %copy-start.61 = (f32[2,1024]{1,0:T(2,128)S(1)}, f32[2,1024]{1,0:T(2,128)}, u32[]{:S(2)}) copy-start(f32[2,1024]{1,0:T(2,128)} %copy-done.60) | copy-start | bytes 24580
  657.1 110.3 %reduce-scatter.17.cloned.1.call-start = ((), (), s32[]{:S(2)}) async-start(), calls=%async_computation.17 | async-start | bytes 5242880 | tf_op jit(solution)/shard_map/reduce_scatter | solution.py:265
  666.3 101.1 %copy-start.4 = (bf16[2,256,1024]{2,1,0:T(8,128)(2,1)S(1)}, bf16[2,256,1024]{2,1,0:T(8,128)(2,1)}, u32[]{:S(2)}) copy-start(bf16[2,256,1024]{2,1,0:T(8,128)(2,1)} %param.14) | copy-start | bytes 3145732
  667.1 101.9 %copy-start.62 = (f32[2,256]{1,0:T(2,128)S(1)}, f32[2,256]{1,0:T(2,128)}, u32[]{:S(2)}) copy-start(f32[2,256]{1,0:T(2,128)} %get-tuple-element.74) | copy-start | bytes 6148
  667.1 101.9 %copy-start.6 = (bf16[2,256,1024]{2,1,0:T(8,128)(2,1)S(1)}, bf16[2,256,1024]{2,1,0:T(8,128)(2,1)}, u32[]{:S(2)}) copy-start(bf16[2,256,1024]{2,1,0:T(8,128)(2,1)} %reduce-scatter.9.cloned.1.call-done) | copy-start | bytes 3145732
  667.1 101.9 %copy-start.8 = (bf16[2,256,1024]{2,1,0:T(8,128)(2,1)S(1)}, bf16[2,256,1024]{2,1,0:T(8,128)(2,1)}, u32[]{:S(2)}) copy-start(bf16[2,256,1024]{2,1,0:T(8,128)(2,1)} %param.27) | copy-start | bytes 3145732
  667.1 101.9 %copy-start.56 = (f32[2,256]{1,0:T(2,128)S(1)}, f32[2,256]{1,0:T(2,128)}, u32[]{:S(2)}) copy-start(f32[2,256]{1,0:T(2,128)} %copy-done.55) | copy-start | bytes 6148
  (45 other events, 194.0 us)
Sparse Core Ops, SparseCore 0:
  13.0 50.6 all-gather.9
  65.2 32.6 all-gather.7
  100.7 79.8 all-gather.11
  183.0 42.6 reduce-scatter.8
  227.8 53.7 all-gather.13
  283.6 32.6 all-gather.17
  318.0 34.4 all-gather.15
  385.4 44.5 reduce-scatter.10
  436.1 34.4 all-gather.19
  473.0 44.5 reduce-scatter.14
  521.7 128.9 reduce-scatter.12
  657.2 63.9 reduce-scatter.18
  723.9 43.4 reduce-scatter.16

commit v3 on v2

--- a/solution.py
+++ b/solution.py
@@ -120,6 +120,37 @@
         * score_scale
     )
     return (query_grad.reshape(seq_len, heads, head_dim), key_grad, value_grad.astype(jnp.bfloat16))
+
+
+def shifted(block, step):
+    parts = lax.axis_size("tensor")
+    return lax.ppermute(block, "tensor", [(place, (place + step) % parts) for place in range(parts)])
+
+
+def gather_positions(mine):
+    parts = lax.axis_size("tensor")
+    place = lax.axis_index("tensor")
+    rows = mine.shape[1]
+    whole = jnp.zeros((mine.shape[0], rows * parts, mine.shape[2]), mine.dtype)
+    for step in range(parts):
+        piece = mine if step == 0 else shifted(mine, step)
+        whole = lax.dynamic_update_slice_in_dim(
+            whole, piece, ((place + parts - step) % parts) * rows, axis=1
+        )
+    return whole
+
+
+def scatter_positions(sums):
+    parts = lax.axis_size("tensor")
+    place = lax.axis_index("tensor")
+    rows = sums.shape[1] // parts
+    total = None
+    for step in range(parts):
+        piece = lax.dynamic_slice_in_dim(sums, ((place + step) % parts) * rows, rows, axis=1)
+        piece = piece if step == 0 else shifted(piece, step)
+        piece = piece.astype(jnp.float32)
+        total = piece if total is None else total + piece
+    return total
 
 
 def each_sequence(attend, packed):
@@ -167,7 +198,7 @@
         [w_query, w_key, w_value, w_out.T, jnp.pad(gain_cols, ((0, 0), (0, 124)))], axis=1
     )
     attn_all = lax.all_gather(attn_pack, "dp", axis=0, tiled=True)
-    tokens_full = lax.all_gather(tokens, "tensor", axis=1, tiled=True)
+    tokens_full = gather_positions(tokens)
     qkv_weight = attn_all[:, :qkv_cols]
     out_weight_t = attn_all[:, qkv_cols : qkv_cols + out_rows]
     gains = attn_all[:, qkv_cols + out_rows : qkv_cols + out_rows + 4].astype(jnp.float32)
@@ -179,7 +210,7 @@
         jnp.concatenate([w_gate, w_up], axis=1), "dp", axis=0, tiled=True
     )
     down_weight_t = lax.all_gather(w_down.T, "dp", axis=0, tiled=True)
-    grad_full = lax.all_gather(out_grad, "tensor", axis=1, tiled=True)
+    grad_full = gather_positions(out_grad)
 
     inputs = tokens.astype(jnp.float32)
     normed = rms_scale(tokens_full.astype(jnp.float32), attn_gain).astype(jnp.bfloat16)
@@ -202,12 +233,7 @@
     mixture, log_total = each_sequence(attend_forward, (queries, key_rows, value_rows, doc_ids))
     attn_sums = project_back(mixture, out_weight_t).astype(jnp.bfloat16)
     attn_sums, gate_up_weight = lax.optimization_barrier((attn_sums, gate_up_weight))
-    attn_out = lax.psum_scatter(
-        attn_sums,
-        "tensor",
-        scatter_dimension=1,
-        tiled=True,
-    ).astype(jnp.float32)
+    attn_out = scatter_positions(attn_sums)
     mid_stream = inputs + attn_out
     normed_mine = rms_scale(mid_stream, ffn_gain).astype(jnp.bfloat16)
     normed_mine, down_weight_t = lax.optimization_barrier((normed_mine, down_weight_t))
@@ -238,7 +264,7 @@
     mid_low = lax.all_gather(mid_grad.astype(jnp.bfloat16), "tensor", axis=1, tiled=True)
     mid_low, ffn_w_grads = lax.optimization_barrier((mid_low, ffn_w_grads))
     ffn_summed = lax.psum_scatter(ffn_w_grads, "dp", scatter_dimension=0, tiled=True)
-    ffn_out = lax.psum_scatter(ffn_sums, "tensor", scatter_dimension=1, tiled=True)
+    ffn_out = scatter_positions(ffn_sums)
     out_w_grad_t = weight_grad(mid_low, mixture)
     mix_grad = project(mid_low, out_weight_t).astype(jnp.bfloat16)
     query_grad, key_grad, value_grad = each_sequence(
@@ -257,17 +283,12 @@
         axis=-1,
     )
     qkv_low, ffn_summed, ffn_out = lax.optimization_barrier((qkv_low, ffn_summed, ffn_out))
-    block_out = (mid_stream + ffn_out.astype(jnp.float32)).astype(jnp.bfloat16)
+    block_out = (mid_stream + ffn_out).astype(jnp.bfloat16)
     input_sums = project_back(qkv_low, qkv_weight)
     attn_gain_grad = jnp.sum(
         input_sums * rms_scale(tokens_full.astype(jnp.float32), 1.0), axis=(0, 1)
     )
-    input_norm_grad = lax.psum_scatter(
-        input_sums.astype(jnp.bfloat16),
-        "tensor",
-        scatter_dimension=1,
-        tiled=True,
-    ).astype(jnp.float32)
+    input_norm_grad = scatter_positions(input_sums.astype(jnp.bfloat16))
     input_pull = jax.vjp(rms_scale, inputs, attn_gain)[1]
     input_grad = input_pull(input_norm_grad)[0]
     tokens_grad = mid_grad + input_grad

time: 787 us -> 685 us (0.87)
  waiting for transfers between devices: 415 us -> 230 us
  blocking collectives: 39.6 us -> 75.7 us
  local copies, waits for them, and re-layouts: 34.5 us -> 57.8 us
  matrix products: 189 us -> 201 us
  starting transfers between devices: 0.52 us -> 11.8 us
    ppermute x0 -> x15, waiting for transfers between devices: none -> 162 us  [shifted(): lax.ppermute(block, 'tensor', [(place, (place + step) % parts) for place...]
    reduce_scatter x3 -> x0, waiting for transfers between devices: 84.9 us -> none  [the longest x1 44.4 us: on_device(): lax.psum_scatter(attn_sums, 'tensor', scatter_dimension=1, tiled=True)]
    reduce_scatter x1, waiting for transfers between devices: 73 us -> 3.57 us  [on_device(): lax.psum_scatter(ffn_w_grads, 'dp', scatter_dimension=0, tiled=True)]
    all_gather x2 -> x0, waiting for transfers between devices: 52.7 us -> none  [the longest x1 33.4 us: on_device(): tokens_full = lax.all_gather(tokens, 'tensor', axis=1, tiled=True)]
    all_gather x1, waiting for transfers between devices: 51.6 us -> 0.01 us  [on_device(): down_weight_t = lax.all_gather(w_down.T, 'dp', axis=0, tiled=True)]
    all_gather x1, waiting for transfers between devices: 43 us -> 0.02 us  [on_device(): attn_all = lax.all_gather(attn_pack, 'dp', axis=0, tiled=True)]
    psum x1, blocking collectives: 39.6 us -> 75.7 us  [on_device(): lax.psum(gain_cut, ('dp', 'tensor'))]
    all_gather x1, waiting for transfers between devices: 33.9 us -> 0.01 us  [on_device(): normed_mid = lax.all_gather(normed_mine, 'tensor', axis=1, tiled=True)]
  transfers between devices with their start and end apart: 13 -> 23, of which waited for: 11 -> 13; matrix products, arithmetic and copies ran while one was open for 31% -> 38% of each run, Pallas kernels for 0% -> 0%
where the time goes in v3:
time: 685 us; the launch traced here: 677 us
  waiting for transfers between devices  230 us (34%)
  matrix products  201 us (29%)
  other arithmetic  85.7 us (13%)
  blocking collectives  75.7 us (11%)
  local copies, waits for them, and re-layouts  57.8 us (8%)
  between operations  15.6 us (2%)
  starting transfers between devices  11.8 us (2%)
    ppermute x15, waiting for transfers between devices, shifted(): lax.ppermute(block, 'tensor', [(place, (place + step) % parts) for place...  162 us
    psum x1, blocking collectives, on_device(): lax.psum(gain_cut, ('dp', 'tensor'))  75.7 us
    reduce_scatter x1, waiting for transfers between devices, on_device(): lax.psum_scatter(project_back(gate_up_grad, gate_up_weight).astype(jnp.bf...  45.5 us
    dot_general x4, matrix products, project(): jnp.einsum('xpo,oh->xph', matmul_operand, weight_matrix, preferred_elemen...  42.9 us
    dot_general x4, matrix products, project_back(): jnp.einsum('yhp,np->yhn', gradient_term, weight_matrix, preferred_element...  34 us
    dot_general x2, matrix products, attend_backward(): jnp.einsum('qkgd,tkd->kgqt', mix_grouped, value_rows, preferred_element_t...  31.1 us
    dot_general x4, matrix products, weight_grad(): jnp.einsum('wba,wbh->ah', matmul_operand, gradient_term, preferred_elemen...  30.9 us
    unnamed x181, local copies, waits for them, and re-layouts  27.9 us
  transfers between devices with their start and end apart: 23, of which 13 were waited for; matrix products, arithmetic and copies ran while one was open for 38% of the time, Pallas kernels for 0%

profile of v3, /device:TPU:0, one launch (start us, length us, event | category | flops | bytes accessed | tf_op | source)
XLA Modules:
  0.0 677.1 jit_solution(1520471701503357823)
XLA Ops:
  15.5 2.6 collective-permute-start.1
  26.2 14.4 %collective-permute-done = bf16[2,256,1024]{2,1,0:T(8,128)(2,1)} collective-permute-done((bf16[2,256,1024]{2,1,0:T(8,128)(2,1)}, bf16[2,256,1024]{2,1,0:T(8,128)(2,1)}, u32[]{:S(2)}, u32[]{:S(2)}) %collective-permute-start) | collective-permute-done | bytes 1048608 | tf_op jit(solution)/shard_map/ppermute | solution.py:127
  43.8 20.0 %collective-permute-done.2 = bf16[2,256,1024]{2,1,0:T(8,128)(2,1)S(1)} collective-permute-done((bf16[2,256,1024]{2,1,0:T(8,128)(2,1)}, bf16[2,256,1024]{2,1,0:T(8,128)(2,1)S(1)}, u32[]{:S(2)}, u32[]{:S(2)}) %collective-permute-start.2) | collective-permute-done | bytes 1048608 | tf_op jit(solution)/shard_map/ppermute | solution.py:127
  67.6 4.9 fusion.111
  81.0 7.6 %fusion.112 = (f32[2,2,1024]{2,1,0:T(2,128)S(1)}, f32[2,2,1024,1024]{2,3,1,0:T(8,128)}) fusion(bf16[1024,2,2,64]{0,3,2,1:T(8,128)(2,1)S(1)} %bitcast.228, bf16[2,1024,2,32]{1,3,2,0:T(8,128)(2,1)S(1)} %get-tuple-element.105, bf16[2,1024,2,32]{1,3,2,0:T(8,128)(2,1)S(1)} %get-tuple-element.104, pred[1024,1024]{0,1:T(8,128)(4,1)S(1)} %copy-done.46), kind=kOutput, calls=%fused_computation.226 | convolution fusion | flops 549974016 | bytes 18890752 | tf_op jit(solution)/shard_map/qkgd,tkd->kgqt/dot_general | solution.py:76
  88.7 8.1 %fusion.7 = f32[2,2,1024]{2,1,0:T(2,128)S(1)} fusion(f32[2,2,1024,1024]{2,3,1,0:T(8,128)} %get-tuple-element.131, f32[2,2,1024]{2,1,0:T(2,128)S(1)} %get-tuple-element.130), kind=kLoop, calls=%fused_computation.19 | loop fusion | flops 8384512 | bytes 16809984 | tf_op jit(solution)/shard_map/reduce_sum | solution.py:88
  96.8 8.0 %fusion.55 = bf16[2,64,2,1024]{3,1,2,0:T(8,128)(2,1)S(1)} fusion(bf16[1024,2,64,1]{0,2,3,1:T(8,128)(2,1)S(1)} %bitcast.235, f32[2,2,1024,1024]{2,3,1,0:T(8,128)} %get-tuple-element.131, f32[2,2,1024]{2,1,0:T(2,128)S(1)} %fusion.7, f32[2,2,1024]{2,1,0:T(2,128)S(1)} %get-tuple-element.130), kind=kOutput, calls=%fused_computation.101 | convolution fusion | flops 549715968 | bytes 17596416 | tf_op jit(solution)/shard_map/kgqt,tkd->qkgd/dot_general | solution.py:90
  105.0 8.6 %fusion.113 = (f32[2,2,1024]{2,1,0:T(2,128)S(1)}, f32[2,2,1024,1024]{2,3,1,0:T(8,128)}) fusion(bf16[1024,2,2,64]{0,3,2,1:T(8,128)(2,1)S(1)} %bitcast.226, bf16[2,1024,2,32]{1,3,2,0:T(8,128)(2,1)S(1)} %get-tuple-element.104, bf16[2,1024,2,32]{1,3,2,0:T(8,128)(2,1)S(1)} %get-tuple-element.105, pred[1024,1024]{0,1:T(8,128)(4,1)} %fusion.32), kind=kOutput, calls=%fused_computation.227 | convolution fusion | flops 549974016 | bytes 18890752 | tf_op jit(solution)/shard_map/qkgd,tkd->kgqt/dot_general | solution.py:76
  113.7 8.0 %fusion.6 = f32[2,2,1024]{2,1,0:T(2,128)S(1)} fusion(f32[2,2,1024,1024]{2,3,1,0:T(8,128)} %get-tuple-element.133, f32[2,2,1024]{2,1,0:T(2,128)S(1)} %get-tuple-element.132), kind=kLoop, calls=%fused_computation.18 | loop fusion | flops 8384512 | bytes 16809984 | tf_op jit(solution)/shard_map/reduce_sum | solution.py:88
  121.7 7.5 %fusion.56 = bf16[2,64,2,1024]{3,1,2,0:T(8,128)(2,1)S(1)} fusion(bf16[1024,2,64,1]{0,2,3,1:T(8,128)(2,1)S(1)} %bitcast.233, f32[2,2,1024,1024]{2,3,1,0:T(8,128)} %get-tuple-element.133, f32[2,2,1024]{2,1,0:T(2,128)S(1)} %fusion.6, f32[2,2,1024]{2,1,0:T(2,128)S(1)} %get-tuple-element.132), kind=kOutput, calls=%fused_computation.102 | convolution fusion | flops 549715968 | bytes 17596416 | tf_op jit(solution)/shard_map/kgqt,tkd->qkgd/dot_general | solution.py:90
  129.4 4.4 convolution_convert_fusion.1
  133.8 10.8 %all-gather.8.cloned.1.call-done = bf16[1024,2304]{1,0:T(8,128)(2,1)} async-done(((bf16[128,2304]{1,0:T(8,128)(2,1)}), bf16[1024,2304]{1,0:T(8,128)(2,1)}) %all-gather.8.cloned.1.call-update) | async-done | bytes 4718608 | tf_op jit(solution)/shard_map/all_gather | solution.py:209
  144.6 3.6 constant_dynamic-slice_fusion.9
  150.0 21.1 %collective-permute-done.5 = bf16[2,256,1024]{2,1,0:T(8,128)(2,1)S(1)} collective-permute-done((bf16[2,256,1024]{2,1,0:T(8,128)(2,1)}, bf16[2,256,1024]{2,1,0:T(8,128)(2,1)S(1)}, u32[]{:S(2)}, u32[]{:S(2)}) %collective-permute-start.5) | collective-permute-done | bytes 1048608 | tf_op jit(solution)/shard_map/ppermute | solution.py:127
  171.1 25.2 %collective-permute-done.4 = bf16[2,256,1024]{2,1,0:T(8,128)(2,1)S(1)} collective-permute-done((bf16[2,256,1024]{2,1,0:T(8,128)(2,1)}, bf16[2,256,1024]{2,1,0:T(8,128)(2,1)S(1)}, u32[]{:S(2)}, u32[]{:S(2)}) %collective-permute-start.4) | collective-permute-done | bytes 1048608 | tf_op jit(solution)/shard_map/ppermute | solution.py:127
  197.4 3.0 multiply_reduce_fusion.2
  203.5 2.5 broadcast.218.clone.1
  207.1 35.8 %collective-permute-done.6 = bf16[2,256,1024]{2,1,0:T(8,128)(2,1)S(1)} collective-permute-done((bf16[2,256,1024]{2,1,0:T(8,128)(2,1)}, bf16[2,256,1024]{2,1,0:T(8,128)(2,1)S(1)}, u32[]{:S(2)}, u32[]{:S(2)}) %collective-permute-start.6) | collective-permute-done | bytes 1048608 | tf_op jit(solution)/shard_map/ppermute | solution.py:127
  246.4 23.2 %collective-permute-done.8 = bf16[2,256,1024]{2,1,0:T(8,128)(2,1)S(1)} collective-permute-done((bf16[2,256,1024]{2,1,0:T(8,128)(2,1)}, bf16[2,256,1024]{2,1,0:T(8,128)(2,1)S(1)}, u32[]{:S(2)}, u32[]{:S(2)}) %collective-permute-start.8) | collective-permute-done | bytes 1048608 | tf_op jit(solution)/shard_map/ppermute | solution.py:127
  270.7 17.2 %fusion.29 = f32[2,1024,2304]{2,1,0:T(8,128)} fusion(bf16[2,1024,1024]{2,1,0:T(8,128)(2,1)} %all-gather.12.cloned.1.call-done, bf16[1024,2304]{1,0:T(8,128)(2,1)} %all-gather.8.cloned.1.call-done), kind=kOutput, calls=%fused_computation.49 | convolution fusion | flops 9663676416 | bytes 27787264 | tf_op jit(solution)/shard_map/xpo,oh->xph/dot_general | solution.py:55
  287.9 18.3 %fusion.14 = (bf16[2,1024,1152]{2,1,0:T(8,128)(2,1)}, bf16[2,1024,1152]{2,1,0:T(8,128)(2,1)}, bf16[2,1024,1152]{2,1,0:T(8,128)(2,1)}) fusion(f32[2,1024,2304]{2,1,0:T(8,128)} %fusion.29, bf16[2,1024,1024]{2,1,0:T(8,128)(2,1)} %constant_dynamic-update-slice_fusion.3, bf16[1024,1152]{0,1:T(8,128)(2,1)S(1)} %copy-done.73), kind=kOutput, calls=%fused_computation.29 | convolution fusion | flops 4869586944 | bytes 39583744 | tf_op jit(solution)/shard_map/xpo,oh->xph/dot_general | solution.py:55
  306.3 15.2 %fusion.37 = bf16[2,1024,1024]{2,1,0:T(8,128)(2,1)} fusion(bf16[1024,2304]{1,0:T(8,128)(2,1)} %all-gather.8.cloned.1.call-done, bf16[2,1024,1152]{2,1,0:T(8,128)(2,1)} %get-tuple-element.81, bf16[2,1024,1152]{2,1,0:T(8,128)(2,1)} %get-tuple-element.80), kind=kOutput, calls=%fused_computation.63 | convolution fusion | flops 9684647936 | bytes 18350080 | tf_op jit(solution)/shard_map/yhp,np->yhn/dot_general | solution.py:61
  321.6 45.5 %reduce-scatter.6.cloned.1.call-done = bf16[2,256,1024]{2,1,0:T(8,128)(2,1)} async-done(((bf16[2,1024,1024]{2,1,0:T(8,128)(2,1)}), bf16[2,256,1024]{2,1,0:T(8,128)(2,1)}) %reduce-scatter.6.cloned.1.call-update) | async-done | bytes 1048592 | tf_op jit(solution)/shard_map/reduce_scatter | solution.py:251
  369.0 2.8 fusion.78
  371.9 8.3 %convolution_convert_fusion = bf16[2,1024,1024]{2,1,0:T(8,128)(2,1)S(1)} fusion(bf16[2,1024,1152]{2,1,0:T(8,128)(2,1)} %get-tuple-element.82, bf16[1024,1152]{0,1:T(8,128)(2,1)} %all-gather.10.cloned.1.call-done), kind=kOutput, calls=%fused_computation.64 | convolution fusion | flops 4833935360 | bytes 11272192 | tf_op jit(solution)/shard_map/yhp,np->yhn/dot_general | solution.py:61
  385.6 15.7 %bitcast_convert_fusion = bf16[1024,2304]{1,0:T(8,128)(2,1)} fusion(bf16[2,1024,1024]{2,1,0:T(8,128)(2,1)S(1)} %copy-done.72, bf16[2,1024,1152]{2,1,0:T(8,128)(2,1)} %get-tuple-element.81, bf16[2,1024,1152]{2,1,0:T(8,128)(2,1)} %get-tuple-element.80), kind=kOutput, calls=%fused_computation.31 | convolution fusion | flops 9684910080 | bytes 18350080 | tf_op jit(solution)/shard_map/wba,wbh->ah/dot_general | solution.py:67
  401.4 8.6 %bitcast_convert_fusion.1 = bf16[1024,1152]{1,0:T(8,128)(2,1)} fusion(bf16[2,1024,1024]{2,1,0:T(8,128)(2,1)} %constant_dynamic-update-slice_fusion.3, bf16[2,1024,1152]{2,1,0:T(8,128)(2,1)S(1)} %bitcast.257), kind=kOutput, calls=%fused_computation.47 | convolution fusion | flops 4833017856 | bytes 11272192 | tf_op jit(solution)/shard_map/wba,wbh->ah/dot_general | solution.py:67
  409.9 6.4 pad_maximum_fusion.1
  416.3 7.9 %all-gather.14.cloned.1.call-done = bf16[2,1024,1024]{2,1,0:T(8,128)(2,1)} async-done(((bf16[2,256,1024]{2,1,0:T(8,128)(2,1)}), bf16[2,1024,1024]{2,1,0:T(8,128)(2,1)}) %all-gather.14.cloned.1.call-update) | async-done | bytes 4194320 | tf_op jit(solution)/shard_map/all_gather | solution.py:264
  426.9 3.2 slice.193
  430.1 19.8 %collective-permute-done.10 = bf16[2,256,1024]{2,1,0:T(8,128)(2,1)} collective-permute-done((bf16[2,256,1024]{2,1,0:T(8,128)(2,1)}, bf16[2,256,1024]{2,1,0:T(8,128)(2,1)}, u32[]{:S(2)}, u32[]{:S(2)}) %collective-permute-start.10) | collective-permute-done | bytes 1048608 | tf_op jit(solution)/shard_map/ppermute | solution.py:127
  449.9 4.0 convert_add_fusion.1
  456.5 15.6 %fusion = (f32[2,2,1024]{2,1,0:T(2,128)S(1)}, f32[2,1024,1024,2]{2,1,3,0:T(8,128)}) fusion(f32[2,2,1024,1024]{2,3,1,0:T(8,128)} %get-tuple-element.131, f32[2,2,1024]{2,1,0:T(2,128)S(1)} %log_add_fusion, bf16[1024,2,64,1]{0,2,3,1:T(8,128)(2,1)S(1)} %bitcast.236, bf16[1024,2,2,64]{0,3,2,1:T(8,128)(2,1)S(1)} %bitcast.220), kind=kOutput, calls=%fused_computation.2 | convolution fusion | flops 549449728 | bytes 34373632 | tf_op jit(solution)/shard_map/qkgd,tkd->kgqt/dot_general | solution.py:101
  473.7 8.3 %fusion.2 = bf16[2,2,1024,1024]{2,3,1,0:T(8,128)(2,1)S(1)} fusion(f32[2,1024,1024,2]{2,1,3,0:T(8,128)} %get-tuple-element.135, f32[2,2,1024,1024]{2,3,1,0:T(8,128)S(1)} %bitcast.214, f32[2,2,1024]{2,1,0:T(2,128)S(1)} %get-tuple-element.134, f32[2,2,1024]{2,1,0:T(2,128)S(1)} %log_add_fusion), kind=kLoop, calls=%fused_computation.4 | loop fusion | flops 16777216 | bytes 41975808 | tf_op jit(solution)/shard_map/convert_element_type | solution.py:110
  482.1 3.5 fusion.66
  485.7 15.5 %fusion.3 = (f32[2,2,1024]{2,1,0:T(2,128)S(1)}, f32[2,1024,1024,2]{2,1,3,0:T(8,128)}) fusion(f32[2,2,1024,1024]{2,3,1,0:T(8,128)} %get-tuple-element.133, f32[2,2,1024]{2,1,0:T(2,128)S(1)} %log_add_fusion.1, bf16[1024,2,64,1]{0,2,3,1:T(8,128)(2,1)S(1)} %bitcast.234, bf16[1024,2,2,64]{0,3,2,1:T(8,128)(2,1)S(1)} %bitcast.218), kind=kOutput, calls=%fused_computation.7 | convolution fusion | flops 549449728 | bytes 34373632 | tf_op jit(solution)/shard_map/qkgd,tkd->kgqt/dot_general | solution.py:101
  502.5 8.9 %fusion.5 = bf16[2,2,1024,1024]{2,3,1,0:T(8,128)(2,1)S(1)} fusion(f32[2,1024,1024,2]{2,1,3,0:T(8,128)} %get-tuple-element.137, f32[2,2,1024,1024]{2,3,1,0:T(8,128)S(1)} %bitcast.216, f32[2,2,1024]{2,1,0:T(2,128)S(1)} %get-tuple-element.136, f32[2,2,1024]{2,1,0:T(2,128)S(1)} %log_add_fusion.1), kind=kLoop, calls=%fused_computation.9 | loop fusion | flops 16777216 | bytes 41975808 | tf_op jit(solution)/shard_map/convert_element_type | solution.py:110
  511.5 2.7 fusion.64
  517.8 5.2 convolution_multiply_fusion
  533.4 8.6 %fusion.67 = bf16[2,64,1024]{2,1,0:T(8,128)(2,1)S(1)} fusion(bf16[1024,2,2,64]{0,3,2,1:T(8,128)(2,1)S(1)} %bitcast.221, f32[2,2,1024,1024]{2,3,1,0:T(8,128)} %get-tuple-element.131, f32[2,2,1024]{2,1,0:T(2,128)S(1)} %log_add_fusion), kind=kOutput, calls=%fused_computation.111 | convolution fusion | flops 545390592 | bytes 17580032 | tf_op jit(solution)/shard_map/kgqt,qkgd->tkd/dot_general | solution.py:104
  542.1 8.8 %fusion.70 = bf16[2,64,1024]{2,1,0:T(8,128)(2,1)S(1)} fusion(bf16[1024,2,2,64]{0,3,2,1:T(8,128)(2,1)S(1)} %bitcast.219, f32[2,2,1024,1024]{2,3,1,0:T(8,128)} %get-tuple-element.133, f32[2,2,1024]{2,1,0:T(2,128)S(1)} %log_add_fusion.1), kind=kOutput, calls=%fused_computation.112 | convolution fusion | flops 545390592 | bytes 17580032 | tf_op jit(solution)/shard_map/kgqt,qkgd->tkd/dot_general | solution.py:104
  553.9 3.6 reduce-scatter.8.cloned.1.call-done
  557.4 5.3 bitcast_convert_fusion.2
  564.0 2.6 copy.130
  566.6 6.0 fusion.17
  579.2 75.7 %psum.7 = f32[8,272]{1,0:T(8,128)S(1)} all-reduce(f32[8,272]{1,0:T(8,128)S(1)} %pad_maximum_fusion.15), channel_id=1, replica_groups=mesh['dp'=8,'tensor'=4] {'dp','tensor'}, use_global_device_ids=true, to_apply=%region_24.25 | all-reduce | flops 2176 | bytes 17408 | tf_op jit(solution)/shard_map/psum | solution.py:311
  658.3 3.1 fusion.50
  661.5 4.5 fusion.49
  (301 shorter events, 91.0 us)
Async XLA Ops:
  7.2 15.8 %copy-start.5 = (bf16[2,256,1024]{2,1,0:T(8,128)(2,1)S(1)}, bf16[2,256,1024]{2,1,0:T(8,128)(2,1)}, u32[]{:S(2)}) copy-start(bf16[2,256,1024]{2,1,0:T(8,128)(2,1)} %param.14) | copy-start | bytes 3145732
  7.2 59.7 %all-gather.6.cloned.1.call-start = ((), (), s32[]{:S(2)}) async-start(), calls=%async_computation.3 | async-start | bytes 2064384 | tf_op jit(solution)/shard_map/all_gather | solution.py:200
  13.0 131.6 %all-gather.8.cloned.1.call-start = ((), (), s32[]{:S(2)}) async-start(), calls=%async_computation.4 | async-start | bytes 5308416 | tf_op jit(solution)/shard_map/all_gather | solution.py:209
  15.0 186.6 %all-gather.10.cloned.1.call-start = ((), (), s32[]{:S(2)}) async-start(), calls=%async_computation.5 | async-start | bytes 2654208 | tf_op jit(solution)/shard_map/all_gather | solution.py:212
  15.0 25.6 %collective-permute-start = (bf16[2,256,1024]{2,1,0:T(8,128)(2,1)}, bf16[2,256,1024]{2,1,0:T(8,128)(2,1)}, u32[]{:S(2)}, u32[]{:S(2)}) collective-permute-start(bf16[2,256,1024]{2,1,0:T(8,128)(2,1)} %param.14), channel_id=1, source_target_pairs={{0,1},{1,2},{2,3},{3,0},{4,5},{5,6},{6,7},{7,4},{8,9},{9,10},{10,1... | collective-permute-start | bytes 3145736 | tf_op jit(solution)/shard_map/ppermute | solution.py:127
  15.5 26.9 %collective-permute-start.1 = (bf16[2,256,1024]{2,1,0:T(8,128)(2,1)}, bf16[2,256,1024]{2,1,0:T(8,128)(2,1)}, u32[]{:S(2)}, u32[]{:S(2)}) collective-permute-start(bf16[2,256,1024]{2,1,0:T(8,128)(2,1)} %param.14), channel_id=1, source_target_pairs={{0,2},{1,3},{2,0},{3,1},{4,6},{5,7},{6,4},{7,5},{8,10},{9,11},{10,... | collective-permute-start | bytes 3145736 | tf_op jit(solution)/shard_map/ppermute | solution.py:127
  18.1 45.7 %collective-permute-start.2 = (bf16[2,256,1024]{2,1,0:T(8,128)(2,1)}, bf16[2,256,1024]{2,1,0:T(8,128)(2,1)S(1)}, u32[]{:S(2)}, u32[]{:S(2)}) collective-permute-start(bf16[2,256,1024]{2,1,0:T(8,128)(2,1)} %param.14), channel_id=1, source_target_pairs={{0,3},{1,0},{2,1},{3,2},{4,7},{5,4},{6,5},{7,6},{8,11},{9,8},{10,9... | collective-permute-start | bytes 3145736 | tf_op jit(solution)/shard_map/ppermute | solution.py:127
  19.5 251.2 %all-gather.12.cloned.1.call-start = ((), (), s32[]{:S(2)}) async-start(), calls=%async_computation.6 | async-start | bytes 5242880 | tf_op jit(solution)/shard_map/all_gather | solution.py:240
  22.3 57.9 %copy-start.14 = (f32[2,1024,32]{1,2,0:T(8,128)}, f32[2,1024,32]{1,2,0:T(8,128)S(1)}, u32[]{:S(2)}) copy-start(f32[2,1024,32]{1,2,0:T(8,128)S(1)} %get-tuple-element.122) | copy-start | bytes 786436
  22.4 57.9 %copy-start.16 = (f32[2,1024,32]{1,2,0:T(8,128)}, f32[2,1024,32]{1,2,0:T(8,128)S(1)}, u32[]{:S(2)}) copy-start(f32[2,1024,32]{1,2,0:T(8,128)S(1)} %get-tuple-element.123) | copy-start | bytes 786436
  75.6 46.1 %copy-start.42 = (bf16[1,1024,128]{1,2,0:T(8,128)(2,1)}, bf16[1,1024,128]{1,2,0:T(8,128)(2,1)S(1)}, u32[]{:S(2)}) copy-start(bf16[1,1024,128]{1,2,0:T(8,128)(2,1)S(1)} %get-tuple-element.100) | copy-start | bytes 786436
  80.4 24.6 %copy-start.29 = (bf16[2,1024,2,32]{1,3,2,0:T(8,128)(2,1)}, bf16[2,1024,2,32]{1,3,2,0:T(8,128)(2,1)S(1)}, u32[]{:S(2)}) copy-start(bf16[2,1024,2,32]{1,3,2,0:T(8,128)(2,1)S(1)} %get-tuple-element.104) | copy-start | bytes 786436
  80.4 24.6 %copy-start.31 = (bf16[2,1024,2,32]{1,3,2,0:T(8,128)(2,1)}, bf16[2,1024,2,32]{1,3,2,0:T(8,128)(2,1)S(1)}, u32[]{:S(2)}) copy-start(bf16[2,1024,2,32]{1,3,2,0:T(8,128)(2,1)S(1)} %get-tuple-element.105) | copy-start | bytes 786436
  80.5 24.5 %copy-start.34 = (bf16[1,1024,4,64]{1,3,2,0:T(8,128)(2,1)}, bf16[1,1024,4,64]{1,3,2,0:T(8,128)(2,1)S(1)}, u32[]{:S(2)}) copy-start(bf16[1,1024,4,64]{1,3,2,0:T(8,128)(2,1)S(1)} %get-tuple-element.108) | copy-start | bytes 1572868
  105.0 24.4 %copy-start.38 = (bf16[1,1024,256]{2,1,0:T(8,128)(2,1)}, bf16[1,1024,256]{2,1,0:T(8,128)(2,1)S(1)}, u32[]{:S(2)}) copy-start(bf16[1,1024,256]{2,1,0:T(8,128)(2,1)S(1)} %copy.83) | copy-start | bytes 1572868
  129.4 18.9 %copy-start.40 = (bf16[1,1024,256]{2,1,0:T(8,128)(2,1)}, bf16[1,1024,256]{2,1,0:T(8,128)(2,1)S(1)}, u32[]{:S(2)}) copy-start(bf16[1,1024,256]{2,1,0:T(8,128)(2,1)S(1)} %copy.82) | copy-start | bytes 1572868
  148.2 22.8 %collective-permute-start.5 = (bf16[2,256,1024]{2,1,0:T(8,128)(2,1)}, bf16[2,256,1024]{2,1,0:T(8,128)(2,1)S(1)}, u32[]{:S(2)}, u32[]{:S(2)}) collective-permute-start(bf16[2,256,1024]{2,1,0:T(8,128)(2,1)} %get-tuple-element.92), channel_id=1, source_target_pairs={{0,3},{1,0},{2,1},{3,2},{4,7},{5,4},{6,5},{7,6},{8,11},{9,8},{10,9... | collective-permute-start | bytes 3145736 | tf_op jit(solution)/shard_map/ppermute | solution.py:127
  148.2 48.1 %collective-permute-start.4 = (bf16[2,256,1024]{2,1,0:T(8,128)(2,1)}, bf16[2,256,1024]{2,1,0:T(8,128)(2,1)S(1)}, u32[]{:S(2)}, u32[]{:S(2)}) collective-permute-start(bf16[2,256,1024]{2,1,0:T(8,128)(2,1)} %get-tuple-element.93), channel_id=1, source_target_pairs={{0,2},{1,3},{2,0},{3,1},{4,6},{5,7},{6,4},{7,5},{8,10},{9,11},{10,... | collective-permute-start | bytes 3145736 | tf_op jit(solution)/shard_map/ppermute | solution.py:127
  149.7 47.6 %collective-permute-start.3 = (bf16[2,256,1024]{2,1,0:T(8,128)(2,1)}, bf16[2,256,1024]{2,1,0:T(8,128)(2,1)}, u32[]{:S(2)}, u32[]{:S(2)}) collective-permute-start(bf16[2,256,1024]{2,1,0:T(8,128)(2,1)} %get-tuple-element.91), channel_id=1, source_target_pairs={{0,1},{1,2},{2,3},{3,0},{4,5},{5,6},{6,7},{7,4},{8,9},{9,10},{10,1... | collective-permute-start | bytes 3145736 | tf_op jit(solution)/shard_map/ppermute | solution.py:127
  171.1 25.3 %copy-start.47 = (bf16[2,256,1024]{2,1,0:T(8,128)(2,1)}, bf16[2,256,1024]{2,1,0:T(8,128)(2,1)S(1)}, u32[]{:S(2)}) copy-start(bf16[2,256,1024]{2,1,0:T(8,128)(2,1)S(1)} %collective-permute-done.5) | copy-start | bytes 3145732
  201.6 165.5 %reduce-scatter.6.cloned.1.call-start = ((), (), s32[]{:S(2)}) async-start(), calls=%async_computation.7 | async-start | bytes 5242880 | tf_op jit(solution)/shard_map/reduce_scatter | solution.py:251
  201.7 41.3 %collective-permute-start.6 = (bf16[2,256,1024]{2,1,0:T(8,128)(2,1)}, bf16[2,256,1024]{2,1,0:T(8,128)(2,1)S(1)}, u32[]{:S(2)}, u32[]{:S(2)}) collective-permute-start(bf16[2,256,1024]{2,1,0:T(8,128)(2,1)} %param.27), channel_id=1, source_target_pairs={{0,1},{1,2},{2,3},{3,0},{4,5},{5,6},{6,7},{7,4},{8,9},{9,10},{10,1... | collective-permute-start | bytes 3145736 | tf_op jit(solution)/shard_map/ppermute | solution.py:127
  201.7 43.6 %collective-permute-start.7 = (bf16[2,256,1024]{2,1,0:T(8,128)(2,1)}, bf16[2,256,1024]{2,1,0:T(8,128)(2,1)S(1)}, u32[]{:S(2)}, u32[]{:S(2)}) collective-permute-start(bf16[2,256,1024]{2,1,0:T(8,128)(2,1)} %param.27), channel_id=1, source_target_pairs={{0,2},{1,3},{2,0},{3,1},{4,6},{5,7},{6,4},{7,5},{8,10},{9,11},{10,... | collective-permute-start | bytes 3145736 | tf_op jit(solution)/shard_map/ppermute | solution.py:127
  201.8 67.9 %collective-permute-start.8 = (bf16[2,256,1024]{2,1,0:T(8,128)(2,1)}, bf16[2,256,1024]{2,1,0:T(8,128)(2,1)S(1)}, u32[]{:S(2)}, u32[]{:S(2)}) collective-permute-start(bf16[2,256,1024]{2,1,0:T(8,128)(2,1)} %param.27), channel_id=1, source_target_pairs={{0,3},{1,0},{2,1},{3,2},{4,7},{5,4},{6,5},{7,6},{8,11},{9,8},{10,9... | collective-permute-start | bytes 3145736 | tf_op jit(solution)/shard_map/ppermute | solution.py:127
  270.7 17.2 %copy-start.73 = (bf16[1024,1152]{0,1:T(8,128)(2,1)S(1)}, bf16[1024,1152]{0,1:T(8,128)(2,1)}, u32[]{:S(2)}) copy-start(bf16[1024,1152]{0,1:T(8,128)(2,1)} %all-gather.10.cloned.1.call-done) | copy-start | bytes 7077892
  321.5 102.8 %all-gather.14.cloned.1.call-start = ((), (), s32[]{:S(2)}) async-start(), calls=%async_computation.8 | async-start | bytes 5242880 | tf_op jit(solution)/shard_map/all_gather | solution.py:264
  371.9 185.6 %reduce-scatter.8.cloned.1.call-start = ((), (), s32[]{:S(2)}) async-start(), calls=%async_computation.9 | async-start | bytes 7962624 | tf_op jit(solution)/shard_map/reduce_scatter | solution.py:266
  384.1 46.0 %collective-permute-start.11 = (bf16[2,256,1024]{2,1,0:T(8,128)(2,1)}, bf16[2,256,1024]{2,1,0:T(8,128)(2,1)S(1)}, u32[]{:S(2)}, u32[]{:S(2)}) collective-permute-start(bf16[2,256,1024]{2,1,0:T(8,128)(2,1)} %get-tuple-element.89), channel_id=1, source_target_pairs={{0,3},{1,0},{2,1},{3,2},{4,7},{5,4},{6,5},{7,6},{8,11},{9,8},{10,9... | collective-permute-start | bytes 3145736 | tf_op jit(solution)/shard_map/ppermute | solution.py:127
  384.1 65.9 %collective-permute-start.10 = (bf16[2,256,1024]{2,1,0:T(8,128)(2,1)}, bf16[2,256,1024]{2,1,0:T(8,128)(2,1)}, u32[]{:S(2)}, u32[]{:S(2)}) collective-permute-start(bf16[2,256,1024]{2,1,0:T(8,128)(2,1)} %get-tuple-element.90), channel_id=1, source_target_pairs={{0,2},{1,3},{2,0},{3,1},{4,6},{5,7},{6,4},{7,5},{8,10},{9,11},{10,... | collective-permute-start | bytes 3145736 | tf_op jit(solution)/shard_map/ppermute | solution.py:127
  385.6 15.7 %slice-start.8 = ((s8[4718592]{0:T(1024)(128)(4,1)}), s8[4194304]{0:T(1024)(128)(4,1)S(1)}, s32[]{:S(2)}) async-start(s8[4718592]{0:T(1024)(128)(4,1)} %bitcast.256), calls=%async_computation.19 | async-start | bytes 8388608
  385.6 15.7 %slice-start.9 = ((s8[4718592]{0:T(1024)(128)(4,1)}), s8[524288]{0:T(1024)(128)(4,1)S(1)}, s32[]{:S(2)}) async-start(s8[4718592]{0:T(1024)(128)(4,1)} %bitcast.256), calls=%async_computation.20 | async-start | bytes 1048576
  385.6 64.3 %collective-permute-start.9 = (bf16[2,256,1024]{2,1,0:T(8,128)(2,1)}, bf16[2,256,1024]{2,1,0:T(8,128)(2,1)}, u32[]{:S(2)}, u32[]{:S(2)}) collective-permute-start(bf16[2,256,1024]{2,1,0:T(8,128)(2,1)} %get-tuple-element.88), channel_id=1, source_target_pairs={{0,1},{1,2},{2,3},{3,0},{4,5},{5,6},{6,7},{7,4},{8,9},{9,10},{10,1... | collective-permute-start | bytes 3145736 | tf_op jit(solution)/shard_map/ppermute | solution.py:127
  424.3 241.8 %reduce-scatter.10.cloned.1.call-start = ((), (), s32[]{:S(2)}) async-start(), calls=%async_computation.10 | async-start | bytes 1769472
  430.1 23.9 %copy-start.70 = (bf16[2,1024,1024]{2,1,0:T(8,128)(2,1)S(1)}, bf16[2,1024,1024]{2,1,0:T(8,128)(2,1)}, u32[]{:S(2)}) copy-start(bf16[2,1024,1024]{2,1,0:T(8,128)(2,1)} %all-gather.14.cloned.1.call-done) | copy-start | bytes 12582916
  456.4 15.7 %copy-start.23 = (bf16[1,1024,256]{1,2,0:T(8,128)(2,1)}, bf16[1,1024,256]{1,2,0:T(8,128)(2,1)S(1)}, u32[]{:S(2)}) copy-start(bf16[1,1024,256]{1,2,0:T(8,128)(2,1)S(1)} %get-tuple-element.107) | copy-start | bytes 1572868
  456.4 29.2 %copy-start.21 = (bf16[1,1024,256]{1,2,0:T(8,128)(2,1)}, bf16[1,1024,256]{1,2,0:T(8,128)(2,1)S(1)}, u32[]{:S(2)}) copy-start(bf16[1,1024,256]{1,2,0:T(8,128)(2,1)S(1)} %get-tuple-element.106) | copy-start | bytes 1572868
  456.4 15.7 %slice-start = ((s8[16777216]{0:T(1024)(128)(4,1)}), s8[4194304]{0:T(1024)(128)(4,1)S(1)}, s32[]{:S(2)}) async-start(s8[16777216]{0:T(1024)(128)(4,1)} %bitcast.213), calls=%async_computation.11 | async-start | bytes 8388608
  456.4 15.7 %slice-start.1 = ((s8[16777216]{0:T(1024)(128)(4,1)}), s8[4194304]{0:T(1024)(128)(4,1)S(1)}, s32[]{:S(2)}) async-start(s8[16777216]{0:T(1024)(128)(4,1)} %bitcast.213), calls=%async_computation.12 | async-start | bytes 8388608
  456.5 15.7 %slice-start.2 = ((s8[16777216]{0:T(1024)(128)(4,1)}), s8[4194304]{0:T(1024)(128)(4,1)S(1)}, s32[]{:S(2)}) async-start(s8[16777216]{0:T(1024)(128)(4,1)} %bitcast.213), calls=%async_computation.13 | async-start | bytes 8388608
  456.5 17.3 %slice-start.3 = ((s8[16777216]{0:T(1024)(128)(4,1)}), s8[4194304]{0:T(1024)(128)(4,1)S(1)}, s32[]{:S(2)}) async-start(s8[16777216]{0:T(1024)(128)(4,1)} %bitcast.213), calls=%async_computation.14 | async-start | bytes 8388608
  485.7 15.5 %slice-start.4 = ((s8[16777216]{0:T(1024)(128)(4,1)}), s8[4194304]{0:T(1024)(128)(4,1)S(1)}, s32[]{:S(2)}) async-start(s8[16777216]{0:T(1024)(128)(4,1)} %bitcast.215), calls=%async_computation.15 | async-start | bytes 8388608
  485.7 15.5 %slice-start.5 = ((s8[16777216]{0:T(1024)(128)(4,1)}), s8[4194304]{0:T(1024)(128)(4,1)S(1)}, s32[]{:S(2)}) async-start(s8[16777216]{0:T(1024)(128)(4,1)} %bitcast.215), calls=%async_computation.16 | async-start | bytes 8388608
  485.7 15.5 %slice-start.6 = ((s8[16777216]{0:T(1024)(128)(4,1)}), s8[4194304]{0:T(1024)(128)(4,1)S(1)}, s32[]{:S(2)}) async-start(s8[16777216]{0:T(1024)(128)(4,1)} %bitcast.215), calls=%async_computation.17 | async-start | bytes 8388608
  485.7 16.8 %slice-start.7 = ((s8[16777216]{0:T(1024)(128)(4,1)}), s8[4194304]{0:T(1024)(128)(4,1)S(1)}, s32[]{:S(2)}) async-start(s8[16777216]{0:T(1024)(128)(4,1)} %bitcast.215), calls=%async_computation.18 | async-start | bytes 8388608
  574.3 84.0 %copy-start.6 = (bf16[2,256,1024]{2,1,0:T(8,128)(2,1)S(1)}, bf16[2,256,1024]{2,1,0:T(8,128)(2,1)}, u32[]{:S(2)}) copy-start(bf16[2,256,1024]{2,1,0:T(8,128)(2,1)} %param.14) | copy-start | bytes 3145732
  574.3 84.0 %collective-permute-start.14 = (bf16[2,256,1024]{2,1,0:T(8,128)(2,1)}, bf16[2,256,1024]{2,1,0:T(8,128)(2,1)}, u32[]{:S(2)}, u32[]{:S(2)}) collective-permute-start(bf16[2,256,1024]{2,1,0:T(8,128)(2,1)} %get-tuple-element.86), channel_id=1, source_target_pairs={{0,3},{1,0},{2,1},{3,2},{4,7},{5,4},{6,5},{7,6},{8,11},{9,8},{10,9... | collective-permute-start | bytes 3145736 | tf_op jit(solution)/shard_map/ppermute | solution.py:127
  574.4 84.0 %collective-permute-start.13 = (bf16[2,256,1024]{2,1,0:T(8,128)(2,1)}, bf16[2,256,1024]{2,1,0:T(8,128)(2,1)}, u32[]{:S(2)}, u32[]{:S(2)}) collective-permute-start(bf16[2,256,1024]{2,1,0:T(8,128)(2,1)} %get-tuple-element.87), channel_id=1, source_target_pairs={{0,2},{1,3},{2,0},{3,1},{4,6},{5,7},{6,4},{7,5},{8,10},{9,11},{10,... | collective-permute-start | bytes 3145736 | tf_op jit(solution)/shard_map/ppermute | solution.py:127
  575.8 82.6 %collective-permute-start.12 = (bf16[2,256,1024]{2,1,0:T(8,128)(2,1)}, bf16[2,256,1024]{2,1,0:T(8,128)(2,1)}, u32[]{:S(2)}, u32[]{:S(2)}) collective-permute-start(bf16[2,256,1024]{2,1,0:T(8,128)(2,1)} %get-tuple-element.85), channel_id=1, source_target_pairs={{0,1},{1,2},{2,3},{3,0},{4,5},{5,6},{6,7},{7,4},{8,9},{9,10},{10,1... | collective-permute-start | bytes 3145736 | tf_op jit(solution)/shard_map/ppermute | solution.py:127
  (59 other events, 260.1 us)
Sparse Core Ops, SparseCore 0:
  13.1 50.5 all-gather.5
  66.5 78.0 all-gather.7
  146.7 51.9 all-gather.9
  201.7 55.3 all-gather.11
  321.6 45.3 reduce-scatter.5
  372.0 52.2 all-gather.13
  428.4 129.0 reduce-scatter.7
  566.7 63.8 reduce-scatter.9
